TPU v7x, 256 devices: a whole 4x4x8 slice. The times are simulated.
256 devices in a mesh: orb: 32 (over x, z_hi, core), grid: 8 (over y, z_lo).
Axes of the slice: x: 4, y: 4, z: 8 (z_hi: 4, z_lo: 2; z = z_hi * 2 + z_lo), core: 2. Of those that a mesh axis runs over, the one named last changes fastest.
Arguments:
- prior: float32 [384, 32, 48, 128], P('orb', 'grid'), may hold values from -6 to 6
- block: float32 [128, 32, 48, 128], P('orb', 'grid'), may hold values from -36 to 36
- potential: float32 [32, 48, 128], P('grid'), may hold values from -1 to 1
- step_len: float32 [128], P('orb'), may hold values from 0.05 to 0.25
Outputs:
- hprior: float32 [384, 32, 48, 128], P('orb', 'grid')
- hblock: float32 [128, 32, 48, 128], P('orb', 'grid')
- ortho: float32 [128, 32, 48, 128], P('orb', 'grid')
All inputs are finite; a program needn't handle non-finite values.
Results may differ from a plain program's by a relative error of at most 0.00012.
Values sent between devices are 32-bit elements; how exact they have to be, the bound alone decides.
No kernel may reach another device: no remote copies, remote signals or barrier semaphores. Data moves between devices by JAX's collectives and lax.ppermute only.
A program may use at most 128 MiB of HBM per device.

v0:
```python
import jax
import jax.numpy as jnp
from jax import lax
from jax.sharding import PartitionSpec as P

near_coef = 4.0 / 3.0
far_coef = -1.0 / 12.0
norm_eps = 1e-06


def with_halo(block, sides, width):
    for axis, dim in sides:
        count = lax.axis_size(axis)
        forward = [(i, i + 1) for i in range(count - 1)]
        forward.append((count - 1, 0))
        backward = [(target, source) for source, target in forward]
        low = lax.ppermute(
            lax.slice_in_dim(block, block.shape[dim] - width, None, axis=dim), axis, forward
        )
        high = lax.ppermute(lax.slice_in_dim(block, 0, width, axis=dim), axis, backward)
        block = jnp.concatenate([low, block, high], axis=dim)
    return block


def hamiltonian(fields, potential):
    padded = with_halo(fields, (("grid", 1),), 2)
    total = -7.5 * fields
    total = total + near_coef * (padded[:, 3:-1] + padded[:, 1:-3])
    total = total + far_coef * (padded[:, 4:] + padded[:, :-4])
    for axis_num in (2, 3):
        total = total + near_coef * (jnp.roll(fields, 1, axis_num) + jnp.roll(fields, -1, axis_num))
        total = total + far_coef * (jnp.roll(fields, 2, axis_num) + jnp.roll(fields, -2, axis_num))
    return -0.5 * total + potential[None] * fields


def contract(left, right, left_dim, right_dim):
    return lax.dot_general(
        left,
        right,
        (((left_dim,), (right_dim,)), ((), ())),
        precision=lax.Precision.HIGHEST,
        preferred_element_type=jnp.float32,
    )


def on_device(prior, block, potential, step_len):
    hprior = hamiltonian(prior, potential)
    hblock = hamiltonian(block, potential)
    trial = block - step_len[:, None, None, None] * hblock
    blk_local = block.shape[0]
    ncells = prior.shape[1] * prior.shape[2] * prior.shape[3] * lax.axis_size("grid")
    flat_prior = prior.reshape(prior.shape[0], -1)
    flat_trial = trial.reshape(blk_local, -1)
    partial_coef = contract(flat_prior, lax.all_gather(flat_trial, "orb", axis=0, tiled=True), 1, 1)
    coeff = lax.psum(partial_coef, "grid") / ncells
    removed = lax.psum_scatter(
        contract(coeff, flat_prior, 0, 0), "orb", scatter_dimension=0, tiled=True
    )
    proj = flat_trial - removed
    sqnorm = lax.psum(jnp.sum(proj * proj, axis=1), "grid") / ncells
    ortho = proj * lax.rsqrt(sqnorm + norm_eps)[:, None]
    return (hprior, hblock, ortho.reshape(block.shape))


def solution(mesh):
    in_specs = (
        P("orb", "grid", None, None),
        P("orb", "grid", None, None),
        P("grid", None, None),
        P("orb"),
    )
    out_specs = (
        P("orb", "grid", None, None),
        P("orb", "grid", None, None),
        P("orb", "grid", None, None),
    )
    return jax.shard_map(
        on_device, mesh=mesh, in_specs=in_specs, out_specs=out_specs, check_vma=False
    )
```

profile of v0, /device:TPU:1, one launch (start us, length us, event | category | flops | bytes accessed | tf_op | source)
XLA Modules:
  0.0 600.3 jit_solution(12607124628695358254)
XLA Ops:
  7.2 1.1 fusion.42
  8.3 2.5 collective-permute-start.3
  10.9 2.5 collective-permute-start.2
  14.3 2.0 collective-permute-done.3
  16.5 3.8 collective-permute-done.2
  20.3 1.4 multiply_subtract_fusion
  21.7 0.9 reshape.21
  22.7 0.4 copy-done
  23.2 0.9 copy.8
  24.2 94.8 %all-gather.3.cloned.1.call-done = f32[32,4,24576]{2,1,0:T(4,128)} async-done(((f32[1,4,24576]{2,1,0:T(4,128)}), f32[32,4,24576]{2,1,0:T(4,128)}) %all-gather.3.cloned.1.call-update) | async-done | bytes 12582928 | tf_op jit(solution)/shard_map/all_gather | solution.py:54
  119.0 13.0 %reshape.22 = f32[128,24576]{1,0:T(8,128)} reshape(f32[32,4,24576]{2,1,0:T(4,128)} %all-gather.3.cloned.1.call-done) | data formatting | bytes 25165824
  132.0 12.4 %convolution_bitcast_fusion = f32[12,128]{0,1:T(8,128)S(1)} fusion(f32[128,24576]{1,0:T(8,128)} %reshape.22, f32[12,24576]{1,0:T(8,128)S(1)} %bitcast.25), kind=kOutput, calls=%fused_computation.20 | convolution fusion | flops 452984832 | bytes 13768704 | tf_op jit(solution)/shard_map/dot_general | solution.py:37
  144.3 33.7 %psum.14 = f32[12,128]{0,1:T(8,128)S(1)} all-reduce(f32[12,128]{0,1:T(8,128)S(1)} %convolution_bitcast_fusion), channel_id=1, replica_groups=mesh['orb'=32,'grid'=8] {'grid'}, use_global_device_ids=true, to_apply=%region_0.1 | all-reduce | flops 1536 | bytes 12288 | tf_op jit(solution)/shard_map/psum | solution.py:55
  178.1 12.3 %fusion.28 = f32[128,24576]{1,0:T(8,128)} fusion(f32[12,24576]{1,0:T(8,128)S(1)} %bitcast.26, f32[12,128]{0,1:T(8,128)S(1)} %psum.14), kind=kOutput, calls=%fused_computation.45 | convolution fusion | flops 452986368 | bytes 13768704 | tf_op jit(solution)/shard_map/dot_general | solution.py:37
  190.4 0.9 fusion.41
  191.3 3.6 collective-permute-start
  194.8 0.6 dynamic-slice
  196.1 0.6 fusion.40
  196.8 1.8 fusion.35
  198.5 1.8 fusion.36
  200.3 1.6 fusion.37
  202.0 1.6 fusion.39
  203.6 1.8 fusion.33
  205.4 1.8 fusion.34
  207.4 7.9 %collective-permute-done = f32[12,2,48,128]{3,2,1,0:T(8,128)} collective-permute-done((f32[12,2,48,128]{3,2,1,0:T(8,128)}, f32[12,2,48,128]{3,2,1,0:T(8,128)}, u32[]{:S(2)}, u32[]{:S(2)}) %collective-permute-start) | collective-permute-done | bytes 589856 | tf_op jit(solution)/shard_map/ppermute | solution.py:20
  215.4 1.1 constant_dynamic-update-slice_fusion
  216.5 350.8 %all-reduce.3.cloned.1.call-done = f32[128,24576]{1,0:T(8,128)} async-done(((f32[128,24576]{1,0:T(8,128)}), f32[128,24576]{1,0:T(8,128)}) %all-reduce.3.cloned.1.call-update) | async-done | bytes 12582928
  567.3 1.5 multiply_reduce_fusion
  568.8 7.9 %fusion.7 = f32[12,4,48,128]{3,2,1,0:T(8,128)} fusion(f32[12,6,48,128]{3,2,1,0:T(8,128)} %copy-done.2, f32[12,6,48,128]{3,2,1,0:T(8,128)S(1)} %constant_dynamic-update-slice_fusion, f32[12,4,47,128]{3,2,1,0:T(8,128)} %get-tuple-element.18, f32[12,4,1,128]{3,2,1,0:T(1,128)} %get-tuple-element.20, f32[12,4,1,128]{3,2,1,0:T(1,128)} %get-tuple-element.19, ...), kind=kLoop, calls=%fused_computation.8 | loop fusion | flops 8847360 | bytes 16613376 | tf_op jit(solution)/shard_map/add | solution.py:33
  576.7 14.6 %psum.15 = f32[4]{0:T(128)S(1)} all-reduce(f32[4]{0:T(128)S(1)} %multiply_reduce_fusion), channel_id=1, replica_groups=mesh['orb'=32,'grid'=8] {'grid'}, use_global_device_ids=true, to_apply=%region_3.4 | all-reduce | flops 4 | bytes 32 | tf_op jit(solution)/shard_map/psum | solution.py:60
  591.3 1.4 multiply_bitcast_fusion
  592.7 0.8 copy.9
  (33 shorter events, 1.5 us)
Async XLA Ops:
  7.2 6.2 %copy-start.1 = (f32[4,4,48,128]{3,2,1,0:T(8,128)S(1)}, f32[4,4,48,128]{3,2,1,0:T(8,128)}, u32[]{:S(2)}) copy-start(f32[4,4,48,128]{3,2,1,0:T(8,128)} %param.5) | copy-start | bytes 1179652
  7.2 111.8 %all-gather.3.cloned.1.call-start = ((), (), s32[]{:S(2)}) async-start(), calls=%async_computation | async-start | bytes 12976128 | tf_op jit(solution)/shard_map/all_gather | solution.py:54
  8.3 8.1 %collective-permute-start.3 = (f32[4,2,48,128]{3,2,1,0:T(8,128)S(1)}, f32[4,2,48,128]{3,2,1,0:T(8,128)S(1)}, u32[]{:S(2)}, u32[]{:S(2)}) collective-permute-start(f32[4,2,48,128]{3,2,1,0:T(8,128)S(1)} %get-tuple-element.26), channel_id=1, source_target_pairs={{0,1},{1,2},{2,3},{3,4},{4,5},{5,6},{6,7},{7,0},{8,9},{9,10},{10,1... | collective-permute-start | bytes 589832 | tf_op jit(solution)/shard_map/ppermute | solution.py:17
  10.9 9.4 %collective-permute-start.2 = (f32[4,2,48,128]{3,2,1,0:T(8,128)S(1)}, f32[4,2,48,128]{3,2,1,0:T(8,128)S(1)}, u32[]{:S(2)}, u32[]{:S(2)}) collective-permute-start(f32[4,2,48,128]{3,2,1,0:T(8,128)S(1)} %get-tuple-element.25), channel_id=1, source_target_pairs={{1,0},{2,1},{3,2},{4,3},{5,4},{6,5},{7,6},{0,7},{9,8},{10,9},{11,1... | collective-permute-start | bytes 589832 | tf_op jit(solution)/shard_map/ppermute | solution.py:20
  14.3 6.0 copy-start.3
  14.3 6.0 copy-start.4
  21.7 1.4 copy-start
  22.6 544.6 %all-reduce.3.cloned.1.call-start = ((), (), s32[]{:S(2)}) async-start(), calls=%async_computation.1 | async-start | bytes 25165824
  190.3 4.5 copy-start.5
  191.3 15.9 %collective-permute-start.1 = (f32[12,2,48,128]{3,2,1,0:T(8,128)S(1)}, f32[12,2,48,128]{3,2,1,0:T(8,128)S(1)}, u32[]{:S(2)}, u32[]{:S(2)}) collective-permute-start(f32[12,2,48,128]{3,2,1,0:T(8,128)S(1)} %get-tuple-element.22), channel_id=1, source_target_pairs={{0,1},{1,2},{2,3},{3,4},{4,5},{5,6},{6,7},{7,0},{8,9},{9,10},{10,1... | collective-permute-start | bytes 1769480 | tf_op jit(solution)/shard_map/ppermute | solution.py:17
  191.3 24.1 %collective-permute-start = (f32[12,2,48,128]{3,2,1,0:T(8,128)}, f32[12,2,48,128]{3,2,1,0:T(8,128)}, u32[]{:S(2)}, u32[]{:S(2)}) collective-permute-start(f32[12,2,48,128]{3,2,1,0:T(8,128)} %get-tuple-element.21), channel_id=1, source_target_pairs={{1,0},{2,1},{3,2},{4,3},{5,4},{6,5},{7,6},{0,7},{9,8},{10,9},{11,1... | collective-permute-start | bytes 1769480 | tf_op jit(solution)/shard_map/ppermute | solution.py:20
  207.4 7.9 %copy-start.2 = (f32[12,6,48,128]{3,2,1,0:T(8,128)}, f32[12,6,48,128]{3,2,1,0:T(8,128)S(1)}, u32[]{:S(2)}) copy-start(f32[12,6,48,128]{3,2,1,0:T(8,128)S(1)} %get-tuple-element.24) | copy-start | bytes 5308420
Sparse Core Ops, SparseCore 0:
  22.8 96.1 all-gather.2
  190.5 376.7 all-reduce.2
where the time goes:
time: 605 us; the launch traced here: 600 us
  waiting for transfers between devices  459 us (76%)
  blocking collectives  48.3 us (8%)
  local copies, waits for them, and re-layouts  32.1 us (5%)
  matrix products  24.6 us (4%)
  between operations  14.9 us (2%)
  other arithmetic  12.2 us (2%)
  starting transfers between devices  8.74 us (1%)
    unnamed x3, waiting for transfers between devices  351 us
    all_gather x1, waiting for transfers between devices, on_device(): lax.all_gather(flat_trial, 'orb', axis=0, tiled=True)  94.8 us
    psum x1, blocking collectives, on_device(): coeff = lax.psum(partial_coef, 'grid') / ncells  33.7 us
    dot_general x2, matrix products, contract(): lax.dot_general(left, right, (((left_dim,), (right_dim,)), ((), ())), pre...  24.6 us
    unnamed x22, local copies, waits for them, and re-layouts  17 us
    psum x1, blocking collectives, on_device(): sqnorm = lax.psum(jnp.sum(proj * proj, axis=1), 'grid') / ncells  14.6 us
  transfers between devices with their start and end apart: 6, of which 5 were waited for; matrix products, arithmetic and copies ran while one was open for 3% of the time, Pallas kernels for 0%

commit v1 on v0

v1 whole, which is shorter than its diff:
```python
import jax
import jax.numpy as jnp
from jax import lax
from jax.experimental import pallas as pl
from jax.experimental.pallas import tpu as pltpu
from jax.sharding import Mesh, PartitionSpec as P

NORM_EPS = 1e-06
ORB = ("x", "zh", "core")
GRID = ("y", "zl")
NORB = 32
NGRID = 8
LANES = 128
HIGHEST = lax.Precision.HIGHEST
VMEM = pl.BlockSpec(memory_space=pltpu.VMEM)
SMEM = pl.BlockSpec(memory_space=pltpu.SMEM)
PARAMS = pltpu.CompilerParams(vmem_limit_bytes=32 * 1024 * 1024)


def call(kernel, out_shape, in_specs, flops, nbytes):
    single = isinstance(out_shape[0], int)
    shapes = [out_shape] if single else list(out_shape)
    outs = pl.pallas_call(
        kernel,
        out_shape=[jax.ShapeDtypeStruct(s, jnp.float32) for s in shapes],
        in_specs=in_specs,
        out_specs=[VMEM] * len(shapes),
        compiler_params=PARAMS,
        cost_estimate=pl.CostEstimate(flops=flops, bytes_accessed=nbytes, transcendentals=0),
    )
    return (lambda *a: outs(*a)[0]) if single else outs


def apply_stencil(layer, below, above, pot):
    near = below[0] + above[0]
    far = below[1] + above[1]
    rows = layer.shape[0]
    near = near + (pltpu.roll(layer, 1, 0) + pltpu.roll(layer, rows - 1, 0))
    far = far + (pltpu.roll(layer, 2, 0) + pltpu.roll(layer, rows - 2, 0))
    near = near + (pltpu.roll(layer, 1, 1) + pltpu.roll(layer, LANES - 1, 1))
    far = far + (pltpu.roll(layer, 2, 1) + pltpu.roll(layer, LANES - 2, 1))
    return (3.75 + pot) * layer - (2.0 / 3.0) * near + (1.0 / 24.0) * far


def orbital_layers(field_ref, low_ref, high_ref, n):
    layers = [low_ref[n, 0], low_ref[n, 1]]
    layers += [field_ref[n, z] for z in range(field_ref.shape[1])]
    layers += [high_ref[n, 0], high_ref[n, 1]]
    return layers


def stencil_layers(layers, pot_ref):
    for z in range(len(layers) - 4):
        c = z + 2
        yield z, apply_stencil(
            layers[c], (layers[c - 1], layers[c - 2]), (layers[c + 1], layers[c + 2]), pot_ref[z]
        )


def prior_kernel(field_ref, low_ref, high_ref, pot_ref, out_ref):
    def step(n, carry):
        layers = orbital_layers(field_ref, low_ref, high_ref, n)
        for z, value in stencil_layers(layers, pot_ref):
            out_ref[n, z] = value
        return carry

    lax.fori_loop(0, field_ref.shape[0], step, 0)


def block_kernel(field_ref, low_ref, high_ref, pot_ref, step_ref, out_ref, packed_ref):
    nz, nx = field_ref.shape[1], field_ref.shape[2]
    rows = nz * nx // NORB
    per_layer = nx // rows
    for n in range(field_ref.shape[0]):
        layers = orbital_layers(field_ref, low_ref, high_ref, n)
        for z, value in stencil_layers(layers, pot_ref):
            out_ref[n, z] = value
            trial = layers[z + 2] - step_ref[n] * value
            for part in range(per_layer):
                packed_ref[z * per_layer + part, n * rows : (n + 1) * rows, :] = trial[
                    part * rows : (part + 1) * rows
                ]


def pack_kernel(field_ref, packed_ref):
    count, total, _ = field_ref.shape
    rows = total // NORB
    for n in range(count):
        for dest in range(NORB):
            packed_ref[dest, n * rows : (n + 1) * rows, :] = field_ref[
                n, dest * rows : (dest + 1) * rows, :
            ]


def make_coef_kernel(nprior, nblk, rows):
    def kernel(prior_ref, trial_ref, out_ref):
        total = jnp.zeros((nprior, nblk), jnp.float32)
        for r in range(rows):
            left = prior_ref[pl.ds(r, nprior, stride=rows), :]
            right = trial_ref[pl.ds(r, nblk, stride=rows), :]
            total += lax.dot_general(
                left, right, (((1,), (1,)), ((), ())),
                precision=HIGHEST, preferred_element_type=jnp.float32,
            )
        out_ref[...] = total

    return kernel


def make_proj_kernel(nprior, nblk, rows):
    def kernel(coef_ref, prior_ref, trial_ref, out_ref):
        coef_t = coef_ref[...].T
        for r in range(rows):
            left = prior_ref[pl.ds(r, nprior, stride=rows), :]
            removed = jnp.dot(
                coef_t, left, precision=HIGHEST, preferred_element_type=jnp.float32
            )
            out_ref[pl.ds(r, nblk, stride=rows), :] = (
                trial_ref[pl.ds(r, nblk, stride=rows), :] - removed
            )

    return kernel


def square_kernel(proj_ref, out_ref):
    count = 4
    rows = proj_ref.shape[1] // count
    value = proj_ref[0]
    total = value * value
    for s in range(1, proj_ref.shape[0]):
        value = proj_ref[s]
        total = total + value * value
    out_ref[...] = jnp.zeros_like(out_ref)
    for n in range(count):
        out_ref[n : n + 1, :] = jnp.sum(total[n * rows : (n + 1) * rows], axis=0, keepdims=True)


def make_scale_kernel(ncells):
    def kernel(proj_ref, parts_ref, out_ref):
        count = out_ref.shape[0]
        rows = proj_ref.shape[1] // count
        total = parts_ref[0]
        for s in range(1, parts_ref.shape[0]):
            total = total + parts_ref[s]
        sqnorm = jnp.sum(total, axis=1, keepdims=True) / ncells
        scale = lax.rsqrt(sqnorm + NORM_EPS)
        for n in range(count):
            factor = jnp.broadcast_to(scale[n : n + 1], (rows, LANES))
            for s in range(proj_ref.shape[0]):
                out_ref[n, s * rows : (s + 1) * rows, :] = (
                    proj_ref[s, n * rows : (n + 1) * rows, :] * factor
                )

    return kernel


def exchange(value, axes):
    return lax.all_to_all(value, axes, 0, 0, tiled=True)


def spread(value, axes, count):
    return exchange(jnp.broadcast_to(value[None], (count,) + value.shape), axes)


def halos(fields):
    forward = [(i, (i + 1) % NGRID) for i in range(NGRID)]
    backward = [(target, source) for source, target in forward]
    low = lax.ppermute(fields[:, -2:], GRID, forward)
    high = lax.ppermute(fields[:, :2], GRID, backward)
    return low, high


def on_device(prior, block, potential, step_len):
    nprior_loc, nz, nx, ny = prior.shape
    nblk_loc = block.shape[0]
    nprior, nblk = nprior_loc * NORB, nblk_loc * NORB
    cells = nz * nx * ny
    ncells = cells * NGRID
    rows = nz * nx // NORB
    size = 4 * cells

    packed = call(
        pack_kernel, (NORB, nprior_loc * rows, LANES), [VMEM], 0, 2 * nprior_loc * size
    )(prior.reshape(nprior_loc, nz * nx, ny))

    blow, bhigh = halos(block)
    plow, phigh = halos(prior)
    prior_cells = exchange(packed, ORB).reshape(nprior * rows, LANES)

    hblock, trial = call(
        block_kernel,
        [block.shape, (NORB, nblk_loc * rows, LANES)],
        [VMEM, VMEM, VMEM, VMEM, SMEM],
        20 * nblk_loc * cells,
        4 * nblk_loc * size,
    )(block, blow, bhigh, potential, step_len)
    trial_cells = exchange(trial, ORB).reshape(nblk * rows, LANES)

    hprior = call(
        prior_kernel, prior.shape, [VMEM] * 4, 20 * nprior_loc * cells, 3 * nprior_loc * size
    )(prior, plow, phigh, potential)

    coef_bytes = 4 * nprior * nblk
    gemm = 2 * nprior * nblk * rows * LANES
    partial = call(
        make_coef_kernel(nprior, nblk, rows), (nprior, nblk), [VMEM] * 2, gemm, 4 * coef_bytes
    )(prior_cells, trial_cells)
    first = 16
    share = exchange(partial.reshape(first, nprior // first, nblk), ("x", "y"))
    share = jnp.sum(share, axis=0)
    share = jnp.sum(spread(share, ("zh", "core", "zl"), 16), axis=0) / ncells
    coeff = spread(share, ("x", "y"), first).reshape(nprior, nblk)

    proj = call(
        make_proj_kernel(nprior, nblk, rows),
        (nblk * rows, LANES),
        [VMEM] * 3,
        gemm,
        6 * coef_bytes,
    )(coeff, prior_cells, trial_cells)
    back = exchange(proj.reshape(NORB, nblk_loc * rows, LANES), ORB)
    squares = call(square_kernel, (8, LANES), [VMEM], 2 * nblk_loc * cells, nblk_loc * size)(back)
    parts = spread(squares, GRID, NGRID)
    ortho = call(
        make_scale_kernel(ncells),
        (nblk_loc, nz * nx, ny),
        [VMEM] * 2,
        nblk_loc * cells,
        2 * nblk_loc * size,
    )(back, parts)
    return hprior, hblock, ortho.reshape(block.shape)


def solution(mesh):
    fine = Mesh(mesh.devices.reshape(4, 4, 2, 4, 2), ORB + GRID)
    fields = P(ORB, GRID, None, None)
    in_specs = (fields, fields, P(GRID, None, None), P(ORB))
    return jax.shard_map(
        on_device, mesh=fine, in_specs=in_specs, out_specs=(fields,) * 3, check_vma=False
    )
```

time: 605 us -> 170 us (0.28)
  waiting for transfers between devices: 459 us -> 53.3 us
  local copies, waits for them, and re-layouts: 32.1 us -> 7 us
  matrix products: 24.6 us -> 0 us
  blocking collectives: 48.3 us -> 70.3 us
  starting transfers between devices: 8.74 us -> 29.1 us
  between operations: 14.9 us -> 0.75 us
  other arithmetic: 12.2 us -> 0.05 us
  Pallas kernels: 0 us -> 9.08 us
    unnamed x3 -> x0, waiting for transfers between devices: 351 us -> none
    all_gather x1 -> x0, waiting for transfers between devices: 94.8 us -> none  [on_device(): lax.all_gather(flat_trial, 'orb', axis=0, tiled=True)]
    all_to_all x0 -> x4, blocking collectives: none -> 70.3 us  [exchange(): return lax.all_to_all(value, axes, 0, 0, tiled=True)]
    psum x2 -> x0, blocking collectives: 48.3 us -> none  [the longest x1 33.7 us: on_device(): coeff = lax.psum(partial_coef, 'grid') / ncells]
    all_to_all x0 -> x3, waiting for transfers between devices: none -> 28.5 us  [exchange(): return lax.all_to_all(value, axes, 0, 0, tiled=True)]
    dot_general x2 -> x0, matrix products: 24.6 us -> none  [contract(): lax.dot_general(left, right, (((left_dim,), (right_dim,)), ((), ())), pre...]
    all_to_all x0 -> x3, starting transfers between devices: none -> 22.6 us  [exchange(): return lax.all_to_all(value, axes, 0, 0, tiled=True)]
    unnamed x22 -> x16, local copies, waits for them, and re-layouts: 17 us -> 4.3 us
  transfers between devices with their start and end apart: 6 -> 7, of which waited for: 5 -> 6; matrix products, arithmetic and copies ran while one was open for 3% -> 1% of each run, Pallas kernels for 0% -> 2%
where the time goes in v1:
time: 170 us
  blocking collectives  70.3 us (41%)
  waiting for transfers between devices  53.3 us (31%)
  starting transfers between devices  29.1 us (17%)
  Pallas kernels  9.08 us (5%)
  local copies, waits for them, and re-layouts  7 us (4%)
    all_to_all x4, blocking collectives, exchange(): return lax.all_to_all(value, axes, 0, 0, tiled=True)  70.3 us
    all_to_all x3, waiting for transfers between devices, exchange(): return lax.all_to_all(value, axes, 0, 0, tiled=True)  28.5 us
    all_to_all x3, starting transfers between devices, exchange(): return lax.all_to_all(value, axes, 0, 0, tiled=True)  22.6 us
    ppermute x2, waiting for transfers between devices, halos(): low = lax.ppermute(fields[:, -2:], GRID, forward)  18.4 us
    pallas_call x6, Pallas kernels, call(): return (lambda *a: outs(*a)[0]) if single else outs  7.18 us
    ppermute x2, starting transfers between devices, halos(): high = lax.ppermute(fields[:, :2], GRID, backward)  6.4 us
    ppermute x2, waiting for transfers between devices, halos(): high = lax.ppermute(fields[:, :2], GRID, backward)  6.4 us
    unnamed x16, local copies, waits for them, and re-layouts  4.3 us
  transfers between devices with their start and end apart: 7, of which 6 were waited for; matrix products, arithmetic and copies ran while one was open for 1% of the time, Pallas kernels for 2%

profile of v1, /device:TPU:1, one launch (start us, length us, event | category | flops | bytes accessed | tf_op | source)
XLA Modules:
  0.0 169.6 jit_solution(15666285313837418419)
XLA Ops:
  0.6 1.1 fusion.1
  1.8 5.0 %collective-permute-start.3 = (f32[4,2,48,128]{3,2,1,0:T(8,128)S(1)}, f32[4,2,48,128]{3,2,1,0:T(8,128)S(1)}, u32[]{:S(2)}, u32[]{:S(2)}) collective-permute-start(f32[4,2,48,128]{3,2,1,0:T(8,128)S(1)} %get-tuple-element.9), channel_id=1, source_target_pairs={{1,0},{2,1},{3,2},{4,3},{5,4},{6,5},{7,6},{0,7},{9,8},{10,9},{11,1... | collective-permute-start | bytes 589832 | tf_op jit(solution)/shard_map/ppermute | solution.py:169
  6.8 3.6 %collective-permute-done.3.high_ref = f32[4,2,48,128]{3,2,1,0:T(8,128)S(1)} collective-permute-done((f32[4,2,48,128]{3,2,1,0:T(8,128)S(1)}, f32[4,2,48,128]{3,2,1,0:T(8,128)S(1)}, u32[]{:S(2)}, u32[]{:S(2)}) %collective-permute-start.3) | collective-permute-done | bytes 196640 | tf_op jit(solution)/shard_map/ppermute | solution.py:169
  10.4 5.3 %collective-permute-done.2.low_ref = f32[4,2,48,128]{3,2,1,0:T(8,128)S(1)} collective-permute-done((f32[4,2,48,128]{3,2,1,0:T(8,128)S(1)}, f32[4,2,48,128]{3,2,1,0:T(8,128)S(1)}, u32[]{:S(2)}, u32[]{:S(2)}) %collective-permute-start.2) | collective-permute-done | bytes 196640 | tf_op jit(solution)/shard_map/ppermute | solution.py:168
  15.6 1.0 copy-done.4
  16.6 0.9 copy-done.5
  17.5 0.7 copy-done.7
  18.2 1.9 %shard_map.68 = (f32[4,4,48,128]{3,2,1,0:T(8,128)}, f32[32,24,128]{2,1,0:T(8,128)}) custom-call(f32[4,4,48,128]{3,2,1,0:T(8,128)S(1)} %copy-done.4, f32[4,2,48,128]{3,2,1,0:T(8,128)S(1)} %collective-permute-done.2.low_ref, f32[4,2,48,128]{3,2,1,0:T(8,128)S(1)} %collective-permute-done.3.high_ref, f32[4,48,128]{2,1,0:T(8,128)S(1)} %copy-done.5, f32[4]{0:T(128)S(1)} %copy-done.7), custom_call_target="tpu_custom_call" | custom-call | flops 1966080 | bytes 1572864 | tf_op jit(solution)/shard_map/pallas_call | solution.py:190
  20.1 12.1 %all-to-all-start.1 = ((f32[32,24,128]{2,1,0:T(8,128)}), f32[32,24,128]{2,1,0:T(8,128)S(1)}, u32[]{:S(2)}, u32[]{:S(2)}) async-start(f32[32,24,128]{2,1,0:T(8,128)} %get-tuple-element.6), calls=%async_computation.1 | async-start | bytes 786432 | tf_op jit(solution)/shard_map/all_to_all | solution.py:158
  32.2 0.1 shard_map.69
  32.4 15.2 %all-to-all-done.1 = f32[32,24,128]{2,1,0:T(8,128)S(1)} async-done(((f32[32,24,128]{2,1,0:T(8,128)}), f32[32,24,128]{2,1,0:T(8,128)S(1)}, u32[]{:S(2)}, u32[]{:S(2)}) %all-to-all-start.1) | async-done | bytes 393248 | tf_op jit(solution)/shard_map/all_to_all | solution.py:158
  47.5 0.7 copy-done.1
  48.3 37.5 %all_to_all.35 = f32[32,72,128]{2,1,0:T(8,128)S(1)} all-to-all(f32[32,72,128]{2,1,0:T(8,128)S(1)} %shard_map.69), channel_id=1, replica_groups=mesh['x'=4,'zh'=4,'core'=2,'y'=4,'zl'=2] {'x','zh','core'}, dimensions={0} | all-to-all | bytes 2359296 | tf_op jit(solution)/shard_map/all_to_all | solution.py:158
  85.8 1.0 copy-done.2
  86.8 1.1 shard_map.70
  88.0 0.0 copy-start.3
  88.0 9.8 %all_to_all.36 = f32[16,24,128]{2,1,0:T(8,128)S(1)} all-to-all(f32[16,24,128]{2,1,0:T(8,128)S(1)} %bitcast.13), channel_id=1, replica_groups=mesh['x'=4,'zh'=4,'core'=2,'y'=4,'zl'=2] {'x','y'}, dimensions={0} | all-to-all | bytes 393216 | tf_op jit(solution)/shard_map/all_to_all | solution.py:158
  97.8 12.7 %all_to_all.37 = f32[16,24,128]{2,1,0:T(8,128)S(1)} all-to-all(f32[16,24,128]{2,1,0:T(8,128)S(1)} %broadcast_in_dim.6), channel_id=1, replica_groups=mesh['x'=4,'zh'=4,'core'=2,'y'=4,'zl'=2] {'zh','core','zl'}, dimensions={0} | all-to-all | bytes 393216 | tf_op jit(solution)/shard_map/all_to_all | solution.py:158
  110.6 10.2 %all_to_all.38 = f32[16,24,128]{2,1,0:T(8,128)S(1)} all-to-all(f32[16,24,128]{2,1,0:T(8,128)S(1)} %broadcast_in_dim.7), channel_id=1, replica_groups=mesh['x'=4,'zh'=4,'core'=2,'y'=4,'zl'=2] {'x','y'}, dimensions={0} | all-to-all | bytes 393216 | tf_op jit(solution)/shard_map/all_to_all | solution.py:158
  120.8 1.9 %shard_map.71 = f32[768,128]{1,0:T(8,128)} custom-call(f32[384,128]{1,0:T(8,128)S(1)} %bitcast.12, f32[2304,128]{1,0:T(8,128)S(1)} %bitcast.9, f32[768,128]{1,0:T(8,128)S(1)} %bitcast.11), custom_call_target="tpu_custom_call" | custom-call | flops 75497472 | bytes 1179648 | tf_op jit(solution)/shard_map/pallas_call | solution.py:31
  122.7 6.6 %all-to-all-start.5 = ((f32[32,24,128]{2,1,0:T(8,128)}), f32[32,24,128]{2,1,0:T(8,128)S(1)}, u32[]{:S(2)}, u32[]{:S(2)}) async-start(f32[32,24,128]{2,1,0:T(8,128)} %bitcast.5), calls=%async_computation.5 | async-start | bytes 786432 | tf_op jit(solution)/shard_map/all_to_all | solution.py:158
  129.3 0.9 fusion
  130.2 1.4 collective-permute-start.1
  131.6 0.1 collective-permute-start
  131.7 13.3 %all-to-all-done.5.proj_ref = f32[32,24,128]{2,1,0:T(8,128)S(1)} async-done(((f32[32,24,128]{2,1,0:T(8,128)}), f32[32,24,128]{2,1,0:T(8,128)S(1)}, u32[]{:S(2)}, u32[]{:S(2)}) %all-to-all-start.5) | async-done | bytes 393248 | tf_op jit(solution)/shard_map/all_to_all | solution.py:158
  145.0 0.1 shard_map.72
  145.1 0.6 broadcast_in_dim.8
  145.7 4.0 %all-to-all-start.6 = ((f32[8,8,128]{2,1,0:T(8,128)}), f32[8,8,128]{2,1,0:T(8,128)S(1)}, u32[]{:S(2)}, u32[]{:S(2)}) async-start(f32[8,8,128]{2,1,0:T(8,128)} %broadcast_in_dim.8), calls=%async_computation.6 | async-start | bytes 65536 | tf_op jit(solution)/shard_map/all_to_all | solution.py:158
  149.6 2.8 %collective-permute-done.1.high_ref = f32[12,2,48,128]{3,2,1,0:T(8,128)S(1)} collective-permute-done((f32[12,2,48,128]{3,2,1,0:T(8,128)}, f32[12,2,48,128]{3,2,1,0:T(8,128)S(1)}, u32[]{:S(2)}, u32[]{:S(2)}) %collective-permute-start.1) | collective-permute-done | bytes 589856 | tf_op jit(solution)/shard_map/ppermute | solution.py:169
  152.5 13.1 %collective-permute-done.low_ref = f32[12,2,48,128]{3,2,1,0:T(8,128)S(1)} collective-permute-done((f32[12,2,48,128]{3,2,1,0:T(8,128)S(1)}, f32[12,2,48,128]{3,2,1,0:T(8,128)S(1)}, u32[]{:S(2)}, u32[]{:S(2)}) %collective-permute-start) | collective-permute-done | bytes 589856 | tf_op jit(solution)/shard_map/ppermute | solution.py:168
  165.6 3.1 %shard_map.67 = f32[12,4,48,128]{3,2,1,0:T(8,128)} custom-call(f32[12,4,48,128]{3,2,1,0:T(8,128)S(1)} %copy-done, f32[12,2,48,128]{3,2,1,0:T(8,128)S(1)} %collective-permute-done.low_ref, f32[12,2,48,128]{3,2,1,0:T(8,128)S(1)} %collective-permute-done.1.high_ref, f32[4,48,128]{2,1,0:T(8,128)S(1)} %copy-done.6), custom_call_target="tpu_custom_call" | custom-call | flops 5898240 | bytes 3538944 | tf_op jit(solution)/shard_map/pallas_call | solution.py:31
  168.7 0.9 shard_map.73
  (17 shorter events, 0.1 us)
Async XLA Ops:
  0.6 31.6 %copy-start = (f32[12,4,48,128]{3,2,1,0:T(8,128)S(1)}, f32[12,4,48,128]{3,2,1,0:T(8,128)}, u32[]{:S(2)}) copy-start(f32[12,4,48,128]{3,2,1,0:T(8,128)} %field_ref.2) | copy-start | bytes 3538948
  1.8 8.6 %collective-permute-start.3 = (f32[4,2,48,128]{3,2,1,0:T(8,128)S(1)}, f32[4,2,48,128]{3,2,1,0:T(8,128)S(1)}, u32[]{:S(2)}, u32[]{:S(2)}) collective-permute-start(f32[4,2,48,128]{3,2,1,0:T(8,128)S(1)} %get-tuple-element.9), channel_id=1, source_target_pairs={{1,0},{2,1},{3,2},{4,3},{5,4},{6,5},{7,6},{0,7},{9,8},{10,9},{11,1... | collective-permute-start | bytes 589832 | tf_op jit(solution)/shard_map/ppermute | solution.py:169
  6.8 8.8 %collective-permute-start.2 = (f32[4,2,48,128]{3,2,1,0:T(8,128)S(1)}, f32[4,2,48,128]{3,2,1,0:T(8,128)S(1)}, u32[]{:S(2)}, u32[]{:S(2)}) collective-permute-start(f32[4,2,48,128]{3,2,1,0:T(8,128)S(1)} %get-tuple-element.10), channel_id=1, source_target_pairs={{0,1},{1,2},{2,3},{3,4},{4,5},{5,6},{6,7},{7,0},{8,9},{9,10},{10,1... | collective-permute-start | bytes 589832 | tf_op jit(solution)/shard_map/ppermute | solution.py:168
  15.6 1.0 copy-start.4
  16.6 0.9 copy-start.5
  17.5 0.7 copy-start.7
  20.1 27.5 %all-to-all-start.1 = ((f32[32,24,128]{2,1,0:T(8,128)}), f32[32,24,128]{2,1,0:T(8,128)S(1)}, u32[]{:S(2)}, u32[]{:S(2)}) async-start(f32[32,24,128]{2,1,0:T(8,128)} %get-tuple-element.6), calls=%async_computation.1 | async-start | bytes 786432 | tf_op jit(solution)/shard_map/all_to_all | solution.py:158
  47.5 0.7 copy-start.1
  85.8 1.0 copy-start.2
  88.0 32.9 %copy-start.3 = (f32[32,24,128]{2,1,0:T(8,128)S(1)}, f32[32,24,128]{2,1,0:T(8,128)}, u32[]{:S(2)}) copy-start(f32[32,24,128]{2,1,0:T(8,128)} %copy-done.1) | copy-start | bytes 1179652
  122.7 22.3 %all-to-all-start.5 = ((f32[32,24,128]{2,1,0:T(8,128)}), f32[32,24,128]{2,1,0:T(8,128)S(1)}, u32[]{:S(2)}, u32[]{:S(2)}) async-start(f32[32,24,128]{2,1,0:T(8,128)} %bitcast.5), calls=%async_computation.5 | async-start | bytes 786432 | tf_op jit(solution)/shard_map/all_to_all | solution.py:158
  129.3 36.3 %copy-start.6 = (f32[4,48,128]{2,1,0:T(8,128)S(1)}, f32[4,48,128]{2,1,0:T(8,128)}, u32[]{:S(2)}) copy-start(f32[4,48,128]{2,1,0:T(8,128)} %pot_ref.3) | copy-start | bytes 294916
  130.2 22.2 %collective-permute-start.1 = (f32[12,2,48,128]{3,2,1,0:T(8,128)}, f32[12,2,48,128]{3,2,1,0:T(8,128)S(1)}, u32[]{:S(2)}, u32[]{:S(2)}) collective-permute-start(f32[12,2,48,128]{3,2,1,0:T(8,128)} %get-tuple-element.7), channel_id=1, source_target_pairs={{1,0},{2,1},{3,2},{4,3},{5,4},{6,5},{7,6},{0,7},{9,8},{10,9},{11,1... | collective-permute-start | bytes 1769480 | tf_op jit(solution)/shard_map/ppermute | solution.py:169
  131.6 34.0 %collective-permute-start = (f32[12,2,48,128]{3,2,1,0:T(8,128)S(1)}, f32[12,2,48,128]{3,2,1,0:T(8,128)S(1)}, u32[]{:S(2)}, u32[]{:S(2)}) collective-permute-start(f32[12,2,48,128]{3,2,1,0:T(8,128)S(1)} %get-tuple-element.8), channel_id=1, source_target_pairs={{0,1},{1,2},{2,3},{3,4},{4,5},{5,6},{6,7},{7,0},{8,9},{9,10},{10,1... | collective-permute-start | bytes 1769480 | tf_op jit(solution)/shard_map/ppermute | solution.py:168
  145.7 23.0 %all-to-all-start.6 = ((f32[8,8,128]{2,1,0:T(8,128)}), f32[8,8,128]{2,1,0:T(8,128)S(1)}, u32[]{:S(2)}, u32[]{:S(2)}) async-start(f32[8,8,128]{2,1,0:T(8,128)} %broadcast_in_dim.8), calls=%async_computation.6 | async-start | bytes 65536 | tf_op jit(solution)/shard_map/all_to_all | solution.py:158

commit v2 on v1

--- a/solution.py
+++ b/solution.py
@@ -6,15 +6,19 @@
 from jax.sharding import Mesh, PartitionSpec as P
 
 NORM_EPS = 1e-06
+NEAR = 2.0 / 3.0
+FAR = 1.0 / 24.0
 ORB = ("x", "zh", "core")
 GRID = ("y", "zl")
 NORB = 32
 NGRID = 8
 LANES = 128
+FORWARD = [(i, (i + 1) % NGRID) for i in range(NGRID)]
+BACKWARD = [(target, source) for source, target in FORWARD]
 HIGHEST = lax.Precision.HIGHEST
 VMEM = pl.BlockSpec(memory_space=pltpu.VMEM)
 SMEM = pl.BlockSpec(memory_space=pltpu.SMEM)
-PARAMS = pltpu.CompilerParams(vmem_limit_bytes=32 * 1024 * 1024)
+PARAMS = pltpu.CompilerParams(vmem_limit_bytes=16 * 1024 * 1024)
 
 
 def call(kernel, out_shape, in_specs, flops, nbytes):
@@ -39,7 +43,7 @@
     far = far + (pltpu.roll(layer, 2, 0) + pltpu.roll(layer, rows - 2, 0))
     near = near + (pltpu.roll(layer, 1, 1) + pltpu.roll(layer, LANES - 1, 1))
     far = far + (pltpu.roll(layer, 2, 1) + pltpu.roll(layer, LANES - 2, 1))
-    return (3.75 + pot) * layer - (2.0 / 3.0) * near + (1.0 / 24.0) * far
+    return (3.75 + pot) * layer - NEAR * near + FAR * far
 
 
 def orbital_layers(field_ref, low_ref, high_ref, n):
@@ -67,33 +71,57 @@
     lax.fori_loop(0, field_ref.shape[0], step, 0)
 
 
-def block_kernel(field_ref, low_ref, high_ref, pot_ref, step_ref, out_ref, packed_ref):
-    nz, nx = field_ref.shape[1], field_ref.shape[2]
+def put(packed_ref, slot, z, layer, nz):
+    rows = nz * layer.shape[0] // NORB
+    per_layer = NORB // nz
+    for part in range(per_layer):
+        packed_ref[z * per_layer + part, slot * rows : (slot + 1) * rows, :] = layer[
+            part * rows : (part + 1) * rows
+        ]
+
+
+def inner_kernel(prior_ref, field_ref, pot_ref, step_ref, packed_ref, copy_ref, inner_ref, steps_ref):
+    nprior, nz, nx, _ = prior_ref.shape
+    nblk = field_ref.shape[0]
+    for n in range(nprior):
+        for z in range(nz):
+            put(packed_ref, n, z, prior_ref[n, z], nz)
+    zero = jnp.zeros((nx, LANES), jnp.float32)
+    for n in range(nblk):
+        layers = [zero, zero] + [field_ref[n, z] for z in range(nz)] + [zero, zero]
+        for z, value in stencil_layers(layers, pot_ref):
+            inner_ref[n, z] = value
+            copy_ref[n, z] = layers[z + 2]
+        steps_ref[n] = jnp.full((8, LANES), step_ref[n], jnp.float32)
+
+
+def outer_kernel(prior_ref, field_ref, inner_ref, steps_ref, low_ref, high_ref, out_ref, packed_ref):
+    nblk, nz, nx, _ = field_ref.shape
     rows = nz * nx // NORB
-    per_layer = nx // rows
-    for n in range(field_ref.shape[0]):
-        layers = orbital_layers(field_ref, low_ref, high_ref, n)
-        for z, value in stencil_layers(layers, pot_ref):
+    nprior = prior_ref.shape[1] // rows
+    for dest in range(NORB):
+        packed_ref[dest, : nprior * rows, :] = prior_ref[dest]
+    for n in range(nblk):
+        edge = {
+            0: FAR * low_ref[n, 0] - NEAR * low_ref[n, 1],
+            1: FAR * low_ref[n, 1],
+            nz - 2: FAR * high_ref[n, 0],
+            nz - 1: FAR * high_ref[n, 1] - NEAR * high_ref[n, 0],
+        }
+        step = jnp.broadcast_to(steps_ref[n, 0:1], (nx, LANES))
+        for z in range(nz):
+            value = inner_ref[n, z] + edge[z]
             out_ref[n, z] = value
-            trial = layers[z + 2] - step_ref[n] * value
-            for part in range(per_layer):
-                packed_ref[z * per_layer + part, n * rows : (n + 1) * rows, :] = trial[
-                    part * rows : (part + 1) * rows
-                ]
-
-
-def pack_kernel(field_ref, packed_ref):
-    count, total, _ = field_ref.shape
-    rows = total // NORB
-    for n in range(count):
-        for dest in range(NORB):
-            packed_ref[dest, n * rows : (n + 1) * rows, :] = field_ref[
-                n, dest * rows : (dest + 1) * rows, :
-            ]
+            put(packed_ref, nprior + n, z, field_ref[n, z] - step * value, nz)
 
 
 def make_coef_kernel(nprior, nblk, rows):
-    def kernel(prior_ref, trial_ref, out_ref):
+    count, split = nprior // NORB * rows, nblk // NORB * rows
+
+    def kernel(cells_ref, out_ref, prior_ref, trial_ref):
+        for s in range(NORB):
+            prior_ref[s * count : (s + 1) * count, :] = cells_ref[s, :count, :]
+            trial_ref[s * split : (s + 1) * split, :] = cells_ref[s, count:, :]
         total = jnp.zeros((nprior, nblk), jnp.float32)
         for r in range(rows):
             left = prior_ref[pl.ds(r, nprior, stride=rows), :]
@@ -158,16 +186,16 @@
     return lax.all_to_all(value, axes, 0, 0, tiled=True)
 
 
-def spread(value, axes, count):
-    return exchange(jnp.broadcast_to(value[None], (count,) + value.shape), axes)
-
-
-def halos(fields):
-    forward = [(i, (i + 1) % NGRID) for i in range(NGRID)]
-    backward = [(target, source) for source, target in forward]
-    low = lax.ppermute(fields[:, -2:], GRID, forward)
-    high = lax.ppermute(fields[:, :2], GRID, backward)
-    return low, high
+def repeat(value, count):
+    return jnp.broadcast_to(value[None], (count,) + value.shape)
+
+
+def edges(fields):
+    return fields[:, -2:], fields[:, :2]
+
+
+def halos(sides):
+    return lax.ppermute(sides[0], GRID, FORWARD), lax.ppermute(sides[1], GRID, BACKWARD)
 
 
 def on_device(prior, block, potential, step_len):
@@ -179,37 +207,47 @@
     rows = nz * nx // NORB
     size = 4 * cells
 
-    packed = call(
-        pack_kernel, (NORB, nprior_loc * rows, LANES), [VMEM], 0, 2 * nprior_loc * size
-    )(prior.reshape(nprior_loc, nz * nx, ny))
-
-    blow, bhigh = halos(block)
-    plow, phigh = halos(prior)
-    prior_cells = exchange(packed, ORB).reshape(nprior * rows, LANES)
-
-    hblock, trial = call(
-        block_kernel,
-        [block.shape, (NORB, nblk_loc * rows, LANES)],
-        [VMEM, VMEM, VMEM, VMEM, SMEM],
+    blow, bhigh = halos(edges(block))
+    prior_rows, field, inner, steps = call(
+        inner_kernel,
+        [
+            (NORB, nprior_loc * rows, LANES),
+            block.shape,
+            block.shape,
+            (nblk_loc, 8, LANES),
+        ],
+        [VMEM] * 3 + [SMEM],
         20 * nblk_loc * cells,
-        4 * nblk_loc * size,
-    )(block, blow, bhigh, potential, step_len)
-    trial_cells = exchange(trial, ORB).reshape(nblk * rows, LANES)
-
-    hprior = call(
-        prior_kernel, prior.shape, [VMEM] * 4, 20 * nprior_loc * cells, 3 * nprior_loc * size
-    )(prior, plow, phigh, potential)
-
+        (2 * nprior_loc + 4 * nblk_loc) * size,
+    )(prior, block, potential, step_len)
+    hblock, packed = call(
+        outer_kernel,
+        [block.shape, (NORB, (nprior_loc + nblk_loc) * rows, LANES)],
+        [VMEM] * 6,
+        4 * nblk_loc * cells,
+        (2 * nprior_loc + 4 * nblk_loc) * size,
+    )(prior_rows, field, inner, steps, blow, bhigh)
+    moved = exchange(packed, ORB)
+
+    low_edge, high_edge = edges(prior)
+    moved, low_edge, high_edge = lax.optimization_barrier((moved, low_edge, high_edge))
     coef_bytes = 4 * nprior * nblk
     gemm = 2 * nprior * nblk * rows * LANES
-    partial = call(
-        make_coef_kernel(nprior, nblk, rows), (nprior, nblk), [VMEM] * 2, gemm, 4 * coef_bytes
-    )(prior_cells, trial_cells)
+    partial, prior_cells, trial_cells = call(
+        make_coef_kernel(nprior, nblk, rows),
+        [(nprior, nblk), (nprior * rows, LANES), (nblk * rows, LANES)],
+        [VMEM],
+        gemm,
+        16 * coef_bytes,
+    )(moved)
     first = 16
-    share = exchange(partial.reshape(first, nprior // first, nblk), ("x", "y"))
-    share = jnp.sum(share, axis=0)
-    share = jnp.sum(spread(share, ("zh", "core", "zl"), 16), axis=0) / ncells
-    coeff = spread(share, ("x", "y"), first).reshape(nprior, nblk)
+    share = jnp.sum(exchange(partial.reshape(first, nprior // first, nblk), ("x", "y")), axis=0)
+    phigh = lax.ppermute(high_edge, GRID, BACKWARD)
+    share, low_edge, phigh = lax.optimization_barrier((share, low_edge, phigh))
+    plow = lax.ppermute(low_edge, GRID, FORWARD)
+    share = jnp.sum(exchange(repeat(share, 16), ("zh", "core", "zl")), axis=0) / ncells
+    coeff = exchange(repeat(share, first), ("x", "y")).reshape(nprior, nblk)
+    coeff, plow = lax.optimization_barrier((coeff, plow))
 
     proj = call(
         make_proj_kernel(nprior, nblk, rows),
@@ -219,15 +257,18 @@
         6 * coef_bytes,
     )(coeff, prior_cells, trial_cells)
     back = exchange(proj.reshape(NORB, nblk_loc * rows, LANES), ORB)
+    hprior = call(
+        prior_kernel, prior.shape, [VMEM] * 4, 20 * nprior_loc * cells, 3 * nprior_loc * size
+    )(prior, plow, phigh, potential)
     squares = call(square_kernel, (8, LANES), [VMEM], 2 * nblk_loc * cells, nblk_loc * size)(back)
-    parts = spread(squares, GRID, NGRID)
+    totals = exchange(repeat(squares, NGRID), GRID)
     ortho = call(
         make_scale_kernel(ncells),
         (nblk_loc, nz * nx, ny),
         [VMEM] * 2,
         nblk_loc * cells,
         2 * nblk_loc * size,
-    )(back, parts)
+    )(back, totals)
     return hprior, hblock, ortho.reshape(block.shape)
 
 

time: 170 us -> 149 us (0.88)
  blocking collectives: 70.3 us -> 50.3 us
  waiting for transfers between devices: 53.3 us -> 48.3 us
  local copies, waits for them, and re-layouts: 7 us -> 10.2 us
    ppermute x4, waiting for transfers between devices: 24.8 us -> 1.89 us  [the longest x1 1.88 us: halos(): lax.ppermute(sides[1], GRID, BACKWARD)]
    all_to_all x4 -> x3, blocking collectives: 70.3 us -> 50.3 us  [exchange(): return lax.all_to_all(value, axes, 0, 0, tiled=True)]
    all_to_all x3, waiting for transfers between devices: 28.5 us -> 46.4 us  [exchange(): return lax.all_to_all(value, axes, 0, 0, tiled=True)]
    ppermute x4, starting transfers between devices: 6.46 us -> 9.67 us  [the longest x1 3.21 us: on_device(): phigh = lax.ppermute(high_edge, GRID, BACKWARD)]
    all_to_all x3, starting transfers between devices: 22.6 us -> 19.8 us  [exchange(): return lax.all_to_all(value, axes, 0, 0, tiled=True)]
    unnamed x16 -> x22, local copies, waits for them, and re-layouts: 4.3 us -> 6.75 us
    pallas_call x6 -> x4, Pallas kernels: 7.18 us -> 6.24 us  [call(): return (lambda *a: outs(*a)[0]) if single else outs]
  transfers between devices with their start and end apart: 7 -> 7, of which waited for: 6 -> 4; matrix products, arithmetic and copies ran while one was open for 1% -> 1% of each run, Pallas kernels for 2% -> 4%
where the time goes in v2:
time: 149 us
  blocking collectives  50.3 us (34%)
  waiting for transfers between devices  48.3 us (32%)
  starting transfers between devices  29.5 us (20%)
  local copies, waits for them, and re-layouts  10.2 us (7%)
  Pallas kernels  9.49 us (6%)
    all_to_all x3, blocking collectives, exchange(): return lax.all_to_all(value, axes, 0, 0, tiled=True)  50.3 us
    all_to_all x3, waiting for transfers between devices, exchange(): return lax.all_to_all(value, axes, 0, 0, tiled=True)  46.4 us
    all_to_all x3, starting transfers between devices, exchange(): return lax.all_to_all(value, axes, 0, 0, tiled=True)  19.8 us
    unnamed x22, local copies, waits for them, and re-layouts  6.75 us
    pallas_call x4, Pallas kernels, call(): return (lambda *a: outs(*a)[0]) if single else outs  6.24 us
    ppermute x1, starting transfers between devices, on_device(): phigh = lax.ppermute(high_edge, GRID, BACKWARD)  3.21 us
  transfers between devices with their start and end apart: 7, of which 4 were waited for; matrix products, arithmetic and copies ran while one was open for 1% of the time, Pallas kernels for 4%

profile of v2, /device:TPU:1, one launch (start us, length us, event | category | flops | bytes accessed | tf_op | source)
XLA Modules:
  0.0 148.6 jit_solution(17758742052457952563)
XLA Ops:
  0.6 1.1 fusion.1
  1.7 2.5 %collective-permute-start = (f32[4,2,48,128]{3,2,1,0:T(8,128)S(1)}, f32[4,2,48,128]{3,2,1,0:T(8,128)S(1)}, u32[]{:S(2)}, u32[]{:S(2)}) collective-permute-start(f32[4,2,48,128]{3,2,1,0:T(8,128)S(1)} %get-tuple-element.40), channel_id=1, source_target_pairs={{0,1},{1,2},{2,3},{3,4},{4,5},{5,6},{6,7},{7,0},{8,9},{9,10},{10,1... | collective-permute-start | bytes 589832 | tf_op jit(solution)/shard_map/ppermute | solution.py:198
  4.2 2.5 %collective-permute-start.1 = (f32[4,2,48,128]{3,2,1,0:T(8,128)S(1)}, f32[4,2,48,128]{3,2,1,0:T(8,128)S(1)}, u32[]{:S(2)}, u32[]{:S(2)}) collective-permute-start(f32[4,2,48,128]{3,2,1,0:T(8,128)S(1)} %get-tuple-element.39), channel_id=1, source_target_pairs={{1,0},{2,1},{3,2},{4,3},{5,4},{6,5},{7,6},{0,7},{9,8},{10,9},{11,1... | collective-permute-start | bytes 589832 | tf_op jit(solution)/shard_map/ppermute | solution.py:198
  6.8 1.3 copy-done
  8.0 1.0 copy-done.3
  9.0 0.9 copy-done.8
  9.9 0.7 copy-done.10
  10.6 1.1 shard_map.67
  11.7 1.9 %collective-permute-done.1.high_ref = f32[4,2,48,128]{3,2,1,0:T(8,128)S(1)} collective-permute-done((f32[4,2,48,128]{3,2,1,0:T(8,128)S(1)}, f32[4,2,48,128]{3,2,1,0:T(8,128)S(1)}, u32[]{:S(2)}, u32[]{:S(2)}) %collective-permute-start.1) | collective-permute-done | bytes 196640 | tf_op jit(solution)/shard_map/ppermute | solution.py:198
  13.6 0.9 shard_map.68
  14.5 1.2 copy-done.2
  15.7 12.8 %all-to-all-start = ((f32[32,96,128]{2,1,0:T(8,128)}), f32[32,96,128]{2,1,0:T(8,128)S(1)}, u32[]{:S(2)}, u32[]{:S(2)}) async-start(f32[32,96,128]{2,1,0:T(8,128)} %copy-done.2), calls=%async_computation | async-start | bytes 3145728 | tf_op jit(solution)/shard_map/all_to_all | solution.py:186
  28.5 1.1 fusion
  29.6 38.0 %all-to-all-done.cells_ref = f32[32,96,128]{2,1,0:T(8,128)S(1)} async-done(((f32[32,96,128]{2,1,0:T(8,128)}), f32[32,96,128]{2,1,0:T(8,128)S(1)}, u32[]{:S(2)}, u32[]{:S(2)}) %all-to-all-start) | async-done | bytes 1572896 | tf_op jit(solution)/shard_map/all_to_all | solution.py:186
  67.6 3.2 %collective-permute-start.2 = (f32[12,2,48,128]{3,2,1,0:T(8,128)}, f32[12,2,48,128]{3,2,1,0:T(8,128)S(1)}, u32[]{:S(2)}, u32[]{:S(2)}) collective-permute-start(f32[12,2,48,128]{3,2,1,0:T(8,128)} %get-tuple-element.28), channel_id=1, source_target_pairs={{1,0},{2,1},{3,2},{4,3},{5,4},{6,5},{7,6},{0,7},{9,8},{10,9},{11,1... | collective-permute-start | bytes 1769480 | tf_op jit(solution)/shard_map/ppermute | solution.py:245
  70.8 1.2 shard_map.69
  72.0 1.0 copy-done.4
  73.0 0.7 copy-done.6
  73.8 12.8 %all_to_all.30 = f32[16,24,128]{2,1,0:T(8,128)S(1)} all-to-all(f32[16,24,128]{2,1,0:T(8,128)S(1)} %bitcast.6), channel_id=1, replica_groups=mesh['x'=4,'zh'=4,'core'=2,'y'=4,'zl'=2] {'x','y'}, dimensions={0} | all-to-all | bytes 393216 | tf_op jit(solution)/shard_map/all_to_all | solution.py:186
  86.6 0.7 broadcast_in_dim.6
  87.3 3.7 %all-to-all-start.2 = ((f32[16,24,128]{2,1,0:T(8,128)}), f32[16,24,128]{2,1,0:T(8,128)S(1)}, u32[]{:S(2)}, u32[]{:S(2)}) async-start(f32[16,24,128]{2,1,0:T(8,128)} %broadcast_in_dim.6), calls=%async_computation.2 | async-start | bytes 393216 | tf_op jit(solution)/shard_map/all_to_all | solution.py:186
  91.0 1.4 collective-permute-start.3
  92.4 7.6 %all-to-all-done.2 = f32[16,24,128]{2,1,0:T(8,128)S(1)} async-done(((f32[16,24,128]{2,1,0:T(8,128)}), f32[16,24,128]{2,1,0:T(8,128)S(1)}, u32[]{:S(2)}, u32[]{:S(2)}) %all-to-all-start.2) | async-done | bytes 196640 | tf_op jit(solution)/shard_map/all_to_all | solution.py:186
  100.0 15.1 %all_to_all.31 = f32[16,24,128]{2,1,0:T(8,128)S(1)} all-to-all(f32[16,24,128]{2,1,0:T(8,128)S(1)} %broadcast_in_dim.7), channel_id=1, replica_groups=mesh['x'=4,'zh'=4,'core'=2,'y'=4,'zl'=2] {'x','y'}, dimensions={0} | all-to-all | bytes 393216 | tf_op jit(solution)/shard_map/all_to_all | solution.py:186
  115.1 1.2 shard_map.71
  116.3 22.4 %all_to_all.32.proj_ref = f32[32,24,128]{2,1,0:T(8,128)S(1)} all-to-all(f32[32,24,128]{2,1,0:T(8,128)S(1)} %bitcast.4), channel_id=1, replica_groups=mesh['x'=4,'zh'=4,'core'=2,'y'=4,'zl'=2] {'x','zh','core'}, dimensions={0} | all-to-all | bytes 786432 | tf_op jit(solution)/shard_map/all_to_all | solution.py:186
  138.7 0.1 shard_map.72
  138.8 0.6 broadcast_in_dim.8
  139.4 3.3 %all-to-all-start.5 = ((f32[8,8,128]{2,1,0:T(8,128)}), f32[8,8,128]{2,1,0:T(8,128)S(1)}, u32[]{:S(2)}, u32[]{:S(2)}) async-start(f32[8,8,128]{2,1,0:T(8,128)} %broadcast_in_dim.8), calls=%async_computation.5 | async-start | bytes 65536 | tf_op jit(solution)/shard_map/all_to_all | solution.py:186
  142.7 4.2 %shard_map.70 = f32[12,4,48,128]{3,2,1,0:T(8,128)} custom-call(f32[12,4,48,128]{3,2,1,0:T(8,128)S(1)} %copy-done.1, f32[12,2,48,128]{3,2,1,0:T(8,128)} %collective-permute-done.3.low_ref, f32[12,2,48,128]{3,2,1,0:T(8,128)S(1)} %collective-permute-done.2.high_ref, f32[4,48,128]{2,1,0:T(8,128)S(1)} %copy-done.9), custom_call_target="tpu_custom_call" | custom-call | flops 5898240 | bytes 3538944 | tf_op jit(solution)/shard_map/pallas_call | solution.py:35
  146.9 0.9 all-to-all-done.5.parts_ref
  147.8 0.9 shard_map.73
  (22 shorter events, 0.1 us)
Async XLA Ops:
  1.7 10.0 %collective-permute-start = (f32[4,2,48,128]{3,2,1,0:T(8,128)S(1)}, f32[4,2,48,128]{3,2,1,0:T(8,128)S(1)}, u32[]{:S(2)}, u32[]{:S(2)}) collective-permute-start(f32[4,2,48,128]{3,2,1,0:T(8,128)S(1)} %get-tuple-element.40), channel_id=1, source_target_pairs={{0,1},{1,2},{2,3},{3,4},{4,5},{5,6},{6,7},{7,0},{8,9},{9,10},{10,1... | collective-permute-start | bytes 589832 | tf_op jit(solution)/shard_map/ppermute | solution.py:198
  4.2 9.4 %collective-permute-start.1 = (f32[4,2,48,128]{3,2,1,0:T(8,128)S(1)}, f32[4,2,48,128]{3,2,1,0:T(8,128)S(1)}, u32[]{:S(2)}, u32[]{:S(2)}) collective-permute-start(f32[4,2,48,128]{3,2,1,0:T(8,128)S(1)} %get-tuple-element.39), channel_id=1, source_target_pairs={{1,0},{2,1},{3,2},{4,3},{5,4},{6,5},{7,6},{0,7},{9,8},{10,9},{11,1... | collective-permute-start | bytes 589832 | tf_op jit(solution)/shard_map/ppermute | solution.py:198
  6.8 1.3 copy-start
  8.0 1.0 copy-start.3
  9.0 0.9 copy-start.8
  9.9 0.7 copy-start.10
  14.5 1.2 copy-start.2
  15.7 12.8 %copy-start.1 = (f32[12,4,48,128]{3,2,1,0:T(8,128)S(1)}, f32[12,4,48,128]{3,2,1,0:T(8,128)}, u32[]{:S(2)}) copy-start(f32[12,4,48,128]{3,2,1,0:T(8,128)} %field_ref.3) | copy-start | bytes 3538948
  15.7 51.9 %all-to-all-start = ((f32[32,96,128]{2,1,0:T(8,128)}), f32[32,96,128]{2,1,0:T(8,128)S(1)}, u32[]{:S(2)}, u32[]{:S(2)}) async-start(f32[32,96,128]{2,1,0:T(8,128)} %copy-done.2), calls=%async_computation | async-start | bytes 3145728 | tf_op jit(solution)/shard_map/all_to_all | solution.py:186
  67.6 19.0 %collective-permute-start.2 = (f32[12,2,48,128]{3,2,1,0:T(8,128)}, f32[12,2,48,128]{3,2,1,0:T(8,128)S(1)}, u32[]{:S(2)}, u32[]{:S(2)}) collective-permute-start(f32[12,2,48,128]{3,2,1,0:T(8,128)} %get-tuple-element.28), channel_id=1, source_target_pairs={{1,0},{2,1},{3,2},{4,3},{5,4},{6,5},{7,6},{0,7},{9,8},{10,9},{11,1... | collective-permute-start | bytes 1769480 | tf_op jit(solution)/shard_map/ppermute | solution.py:245
  72.0 1.0 copy-start.4
  73.0 0.7 copy-start.6
  73.8 41.3 %copy-start.5 = (f32[2304,128]{1,0:T(8,128)S(1)}, f32[2304,128]{1,0:T(8,128)}, u32[]{:S(2)}) copy-start(f32[2304,128]{1,0:T(8,128)} %copy-done.4) | copy-start | bytes 3538948
  73.8 41.3 %copy-start.7 = (f32[768,128]{1,0:T(8,128)S(1)}, f32[768,128]{1,0:T(8,128)}, u32[]{:S(2)}) copy-start(f32[768,128]{1,0:T(8,128)} %copy-done.6) | copy-start | bytes 1179652
  87.3 12.6 %all-to-all-start.2 = ((f32[16,24,128]{2,1,0:T(8,128)}), f32[16,24,128]{2,1,0:T(8,128)S(1)}, u32[]{:S(2)}, u32[]{:S(2)}) async-start(f32[16,24,128]{2,1,0:T(8,128)} %broadcast_in_dim.6), calls=%async_computation.2 | async-start | bytes 393216 | tf_op jit(solution)/shard_map/all_to_all | solution.py:186
  91.0 24.1 %collective-permute-start.3 = (f32[12,2,48,128]{3,2,1,0:T(8,128)}, f32[12,2,48,128]{3,2,1,0:T(8,128)}, u32[]{:S(2)}, u32[]{:S(2)}) collective-permute-start(f32[12,2,48,128]{3,2,1,0:T(8,128)} %get-tuple-element.30), channel_id=1, source_target_pairs={{0,1},{1,2},{2,3},{3,4},{4,5},{5,6},{6,7},{7,0},{8,9},{9,10},{10,1... | collective-permute-start | bytes 1769480 | tf_op jit(solution)/shard_map/ppermute | solution.py:247
  116.2 26.5 %copy-start.9 = (f32[4,48,128]{2,1,0:T(8,128)S(1)}, f32[4,48,128]{2,1,0:T(8,128)}, u32[]{:S(2)}) copy-start(f32[4,48,128]{2,1,0:T(8,128)} %pot_ref.3) | copy-start | bytes 294916
  139.4 8.4 %all-to-all-start.5 = ((f32[8,8,128]{2,1,0:T(8,128)}), f32[8,8,128]{2,1,0:T(8,128)S(1)}, u32[]{:S(2)}, u32[]{:S(2)}) async-start(f32[8,8,128]{2,1,0:T(8,128)} %broadcast_in_dim.8), calls=%async_computation.5 | async-start | bytes 65536 | tf_op jit(solution)/shard_map/all_to_all | solution.py:186

commit v3 on v2

--- a/solution.py
+++ b/solution.py
@@ -15,6 +15,8 @@
 LANES = 128
 FORWARD = [(i, (i + 1) % NGRID) for i in range(NGRID)]
 BACKWARD = [(target, source) for source, target in FORWARD]
+SWAP = [(0, 1), (1, 0)]
+ALONG = [(i, (i + (NGRID - 2 if i % 2 else 2)) % NGRID) for i in range(NGRID)]
 HIGHEST = lax.Precision.HIGHEST
 VMEM = pl.BlockSpec(memory_space=pltpu.VMEM)
 SMEM = pl.BlockSpec(memory_space=pltpu.SMEM)
@@ -46,13 +48,6 @@
     return (3.75 + pot) * layer - NEAR * near + FAR * far
 
 
-def orbital_layers(field_ref, low_ref, high_ref, n):
-    layers = [low_ref[n, 0], low_ref[n, 1]]
-    layers += [field_ref[n, z] for z in range(field_ref.shape[1])]
-    layers += [high_ref[n, 0], high_ref[n, 1]]
-    return layers
-
-
 def stencil_layers(layers, pot_ref):
     for z in range(len(layers) - 4):
         c = z + 2
@@ -61,9 +56,15 @@
         )
 
 
-def prior_kernel(field_ref, low_ref, high_ref, pot_ref, out_ref):
+def prior_kernel(field_ref, near_ref, wrapped_ref, pot_ref, out_ref):
+    upper = lax.axis_index("zl") == 1
+
     def step(n, carry):
-        layers = orbital_layers(field_ref, low_ref, high_ref, n)
+        near = [near_ref[n, z] for z in range(2)]
+        wrapped = [wrapped_ref[n, z] for z in range(2)]
+        low = [jnp.where(upper, near[z], wrapped[z]) for z in range(2)]
+        high = [jnp.where(upper, wrapped[z], near[z]) for z in range(2)]
+        layers = low + [field_ref[n, z] for z in range(field_ref.shape[1])] + high
         for z, value in stencil_layers(layers, pot_ref):
             out_ref[n, z] = value
         return carry
@@ -80,12 +81,20 @@
         ]
 
 
-def inner_kernel(prior_ref, field_ref, pot_ref, step_ref, packed_ref, copy_ref, inner_ref, steps_ref):
+def inner_kernel(
+    prior_ref, field_ref, pot_ref, step_ref,
+    packed_ref, near_ref, far_ref, copy_ref, inner_ref, steps_ref,
+):
     nprior, nz, nx, _ = prior_ref.shape
     nblk = field_ref.shape[0]
+    upper = lax.axis_index("zl") == 1
     for n in range(nprior):
         for z in range(nz):
             put(packed_ref, n, z, prior_ref[n, z], nz)
+        for z in range(2):
+            top, bottom = prior_ref[n, nz - 2 + z], prior_ref[n, z]
+            near_ref[n, z] = jnp.where(upper, bottom, top)
+            far_ref[n, z] = jnp.where(upper, top, bottom)
     zero = jnp.zeros((nx, LANES), jnp.float32)
     for n in range(nblk):
         layers = [zero, zero] + [field_ref[n, z] for z in range(nz)] + [zero, zero]
@@ -208,10 +217,12 @@
     size = 4 * cells
 
     blow, bhigh = halos(edges(block))
-    prior_rows, field, inner, steps = call(
+    prior_rows, near, wrapped, field, inner, steps = call(
         inner_kernel,
         [
             (NORB, nprior_loc * rows, LANES),
+            (nprior_loc, 2, nx, ny),
+            (nprior_loc, 2, nx, ny),
             block.shape,
             block.shape,
             (nblk_loc, 8, LANES),
@@ -229,8 +240,7 @@
     )(prior_rows, field, inner, steps, blow, bhigh)
     moved = exchange(packed, ORB)
 
-    low_edge, high_edge = edges(prior)
-    moved, low_edge, high_edge = lax.optimization_barrier((moved, low_edge, high_edge))
+    moved, near, wrapped = lax.optimization_barrier((moved, near, wrapped))
     coef_bytes = 4 * nprior * nblk
     gemm = 2 * nprior * nblk * rows * LANES
     partial, prior_cells, trial_cells = call(
@@ -241,13 +251,13 @@
         16 * coef_bytes,
     )(moved)
     first = 16
+    near = lax.ppermute(near, "zl", SWAP)
     share = jnp.sum(exchange(partial.reshape(first, nprior // first, nblk), ("x", "y")), axis=0)
-    phigh = lax.ppermute(high_edge, GRID, BACKWARD)
-    share, low_edge, phigh = lax.optimization_barrier((share, low_edge, phigh))
-    plow = lax.ppermute(low_edge, GRID, FORWARD)
+    share, near = lax.optimization_barrier((share, near))
     share = jnp.sum(exchange(repeat(share, 16), ("zh", "core", "zl")), axis=0) / ncells
+    share, wrapped = lax.optimization_barrier((share, wrapped))
+    wrapped = lax.ppermute(wrapped, "zl", SWAP)
     coeff = exchange(repeat(share, first), ("x", "y")).reshape(nprior, nblk)
-    coeff, plow = lax.optimization_barrier((coeff, plow))
 
     proj = call(
         make_proj_kernel(nprior, nblk, rows),
@@ -256,10 +266,12 @@
         gemm,
         6 * coef_bytes,
     )(coeff, prior_cells, trial_cells)
+    proj, wrapped = lax.optimization_barrier((proj, wrapped))
+    wrapped = lax.ppermute(wrapped, GRID, ALONG)
     back = exchange(proj.reshape(NORB, nblk_loc * rows, LANES), ORB)
     hprior = call(
         prior_kernel, prior.shape, [VMEM] * 4, 20 * nprior_loc * cells, 3 * nprior_loc * size
-    )(prior, plow, phigh, potential)
+    )(prior, near, wrapped, potential)
     squares = call(square_kernel, (8, LANES), [VMEM], 2 * nblk_loc * cells, nblk_loc * size)(back)
     totals = exchange(repeat(squares, NGRID), GRID)
     ortho = call(

time: 149 us -> 144 us (0.966)
  blocking collectives: 50.3 us -> 85.5 us
  waiting for transfers between devices: 48.3 us -> 24.7 us
  starting transfers between devices: 29.5 us -> 17.2 us
  local copies, waits for them, and re-layouts: 10.2 us -> 5.52 us
    all_to_all x3 -> x4, blocking collectives: 50.3 us -> 85.5 us  [exchange(): return lax.all_to_all(value, axes, 0, 0, tiled=True)]
    all_to_all x3 -> x2, waiting for transfers between devices: 46.4 us -> 17.2 us  [exchange(): return lax.all_to_all(value, axes, 0, 0, tiled=True)]
    all_to_all x3 -> x2, starting transfers between devices: 19.8 us -> 9.64 us  [exchange(): return lax.all_to_all(value, axes, 0, 0, tiled=True)]
    ppermute x1, waiting for transfers between devices: 0.01 us -> 3.82 us  [halos(): lax.ppermute(sides[0], GRID, FORWARD)]
    ppermute x2 -> x3, waiting for transfers between devices: 0.01 us -> 3.63 us  [the longest x1 2.44 us: on_device(): near = lax.ppermute(near, 'zl', SWAP)]
    unnamed x22 -> x12, local copies, waits for them, and re-layouts: 6.75 us -> 3.82 us
    ppermute x1, starting transfers between devices: 2.54 us -> 0.01 us  [halos(): lax.ppermute(sides[0], GRID, FORWARD)]
    ppermute x1, starting transfers between devices: 2.54 us -> 4.99 us  [halos(): lax.ppermute(sides[1], GRID, BACKWARD)]
  transfers between devices with their start and end apart: 7 -> 7, of which waited for: 4 -> 5; matrix products, arithmetic and copies ran while one was open for 1% -> 0% of each run, Pallas kernels for 4% -> 5%
where the time goes in v3:
time: 144 us; the launch traced here: 143 us
  blocking collectives  85.5 us (59%)
  waiting for transfers between devices  24.7 us (17%)
  starting transfers between devices  17.2 us (12%)
  Pallas kernels  9.27 us (6%)
  local copies, waits for them, and re-layouts  5.52 us (4%)
    all_to_all x4, blocking collectives, exchange(): return lax.all_to_all(value, axes, 0, 0, tiled=True)  85.5 us
    all_to_all x2, waiting for transfers between devices, exchange(): return lax.all_to_all(value, axes, 0, 0, tiled=True)  17.2 us
    all_to_all x2, starting transfers between devices, exchange(): return lax.all_to_all(value, axes, 0, 0, tiled=True)  9.64 us
    pallas_call x4, Pallas kernels, call(): return (lambda *a: outs(*a)[0]) if single else outs  5.92 us
    ppermute x1, starting transfers between devices, halos(): lax.ppermute(sides[1], GRID, BACKWARD)  4.99 us
    ppermute x1, waiting for transfers between devices, halos(): lax.ppermute(sides[0], GRID, FORWARD)  3.82 us
    unnamed x12, local copies, waits for them, and re-layouts  3.82 us
  transfers between devices with their start and end apart: 7, of which 5 were waited for; matrix products, arithmetic and copies ran while one was open for 0% of the time, Pallas kernels for 5%

profile of v3, /device:TPU:1, one launch (start us, length us, event | category | flops | bytes accessed | tf_op | source)
XLA Modules:
  0.0 143.0 jit_solution(11013261422988822803)
XLA Ops:
  0.6 1.1 fusion
  1.7 5.0 %collective-permute-start.1 = (f32[4,2,48,128]{3,2,1,0:T(8,128)S(1)}, f32[4,2,48,128]{3,2,1,0:T(8,128)S(1)}, u32[]{:S(2)}, u32[]{:S(2)}) collective-permute-start(f32[4,2,48,128]{3,2,1,0:T(8,128)S(1)} %get-tuple-element.43), channel_id=1, source_target_pairs={{1,0},{2,1},{3,2},{4,3},{5,4},{6,5},{7,6},{0,7},{9,8},{10,9},{11,1... | collective-permute-start | bytes 589832 | tf_op jit(solution)/shard_map/ppermute | solution.py:207
  6.7 0.0 collective-permute-start
  6.7 1.3 copy-done
  8.0 1.0 copy-done.2
  9.0 0.9 copy-done.3
  9.8 0.7 copy-done.5
  10.5 1.2 shard_map.67
  11.7 0.0 collective-permute-done.1.high_ref
  11.7 3.8 %collective-permute-done.low_ref = f32[4,2,48,128]{3,2,1,0:T(8,128)S(1)} collective-permute-done((f32[4,2,48,128]{3,2,1,0:T(8,128)S(1)}, f32[4,2,48,128]{3,2,1,0:T(8,128)S(1)}, u32[]{:S(2)}, u32[]{:S(2)}) %collective-permute-start) | collective-permute-done | bytes 196640 | tf_op jit(solution)/shard_map/ppermute | solution.py:207
  15.5 0.9 shard_map.68
  16.5 52.2 %all_to_all.30.cells_ref = f32[32,96,128]{2,1,0:T(8,128)S(1)} all-to-all(f32[32,96,128]{2,1,0:T(8,128)S(1)} %get-tuple-element.27), channel_id=1, replica_groups=mesh['x'=4,'zh'=4,'core'=2,'y'=4,'zl'=2] {'x','zh','core'}, dimensions={0} | all-to-all | bytes 3145728 | tf_op jit(solution)/shard_map/all_to_all | solution.py:195
  68.7 1.0 collective-permute-start.2
  69.7 1.2 shard_map.69
  71.0 9.7 %all_to_all.31 = f32[16,24,128]{2,1,0:T(8,128)S(1)} all-to-all(f32[16,24,128]{2,1,0:T(8,128)S(1)} %bitcast.5), channel_id=1, replica_groups=mesh['x'=4,'zh'=4,'core'=2,'y'=4,'zl'=2] {'x','y'}, dimensions={0} | all-to-all | bytes 393216 | tf_op jit(solution)/shard_map/all_to_all | solution.py:195
  80.7 2.4 %collective-permute-done.2.near_ref = f32[12,2,48,128]{3,2,1,0:T(8,128)S(1)} collective-permute-done((f32[12,2,48,128]{3,2,1,0:T(8,128)S(1)}, f32[12,2,48,128]{3,2,1,0:T(8,128)S(1)}, u32[]{:S(2)}, u32[]{:S(2)}) %collective-permute-start.2) | collective-permute-done | bytes 589856 | tf_op jit(solution)/shard_map/ppermute | solution.py:254
  83.2 13.5 %all_to_all.32 = f32[16,24,128]{2,1,0:T(8,128)S(1)} all-to-all(f32[16,24,128]{2,1,0:T(8,128)S(1)} %broadcast_in_dim.6), channel_id=1, replica_groups=mesh['x'=4,'zh'=4,'core'=2,'y'=4,'zl'=2] {'zh','core','zl'}, dimensions={0} | all-to-all | bytes 393216 | tf_op jit(solution)/shard_map/all_to_all | solution.py:195
  96.7 1.5 %collective-permute-start.3 = (f32[12,2,48,128]{3,2,1,0:T(8,128)S(1)}, f32[12,2,48,128]{3,2,1,0:T(8,128)S(1)}, u32[]{:S(2)}, u32[]{:S(2)}) collective-permute-start(f32[12,2,48,128]{3,2,1,0:T(8,128)S(1)} %get-tuple-element.39), channel_id=1, source_target_pairs={{0,1},{1,0},{2,3},{3,2},{4,5},{5,4},{6,7},{7,6},{8,9},{9,8},{10,11... | collective-permute-start | bytes 1769480 | tf_op jit(solution)/shard_map/ppermute | solution.py:259
  98.2 10.0 %all_to_all.33 = f32[16,24,128]{2,1,0:T(8,128)S(1)} all-to-all(f32[16,24,128]{2,1,0:T(8,128)S(1)} %broadcast_in_dim.7), channel_id=1, replica_groups=mesh['x'=4,'zh'=4,'core'=2,'y'=4,'zl'=2] {'x','y'}, dimensions={0} | all-to-all | bytes 393216 | tf_op jit(solution)/shard_map/all_to_all | solution.py:195
  108.3 1.9 %shard_map.70 = f32[768,128]{1,0:T(8,128)} custom-call(f32[384,128]{1,0:T(8,128)S(1)} %bitcast.4, f32[2304,128]{1,0:T(8,128)S(1)} %get-tuple-element.37.prior_ref, f32[768,128]{1,0:T(8,128)S(1)} %get-tuple-element.38.trial_ref), custom_call_target="tpu_custom_call" | custom-call | flops 75497472 | bytes 1179648 | tf_op jit(solution)/shard_map/pallas_call | solution.py:37
  110.2 1.2 collective-permute-done.3
  111.4 6.2 %all-to-all-start.4 = ((f32[32,24,128]{2,1,0:T(8,128)}), f32[32,24,128]{2,1,0:T(8,128)S(1)}, u32[]{:S(2)}, u32[]{:S(2)}) async-start(f32[32,24,128]{2,1,0:T(8,128)} %bitcast.2), calls=%async_computation.4 | async-start | bytes 786432 | tf_op jit(solution)/shard_map/all_to_all | solution.py:195
  117.5 0.1 collective-permute-start.4
  117.6 15.3 %all-to-all-done.4.proj_ref = f32[32,24,128]{2,1,0:T(8,128)S(1)} async-done(((f32[32,24,128]{2,1,0:T(8,128)}), f32[32,24,128]{2,1,0:T(8,128)S(1)}, u32[]{:S(2)}, u32[]{:S(2)}) %all-to-all-start.4) | async-done | bytes 393248 | tf_op jit(solution)/shard_map/all_to_all | solution.py:195
  132.9 0.1 shard_map.72
  132.9 0.6 broadcast_in_dim.8
  133.6 3.5 %all-to-all-start.5 = ((f32[8,8,128]{2,1,0:T(8,128)}), f32[8,8,128]{2,1,0:T(8,128)S(1)}, u32[]{:S(2)}, u32[]{:S(2)}) async-start(f32[8,8,128]{2,1,0:T(8,128)} %broadcast_in_dim.8), calls=%async_computation.5 | async-start | bytes 65536 | tf_op jit(solution)/shard_map/all_to_all | solution.py:195
  137.0 0.0 collective-permute-done.4.wrapped_ref
  137.0 0.0 copy-done.1
  137.1 3.1 %shard_map.71 = f32[12,4,48,128]{3,2,1,0:T(8,128)} custom-call(f32[12,4,48,128]{3,2,1,0:T(8,128)S(1)} %copy-done.1, f32[12,2,48,128]{3,2,1,0:T(8,128)S(1)} %collective-permute-done.2.near_ref, f32[12,2,48,128]{3,2,1,0:T(8,128)S(1)} %collective-permute-done.4.wrapped_ref, f32[4,48,128]{2,1,0:T(8,128)S(1)} %copy-done.4), custom_call_target="tpu_custom_call" | custom-call | flops 5898240 | bytes 3538944 | tf_op jit(solution)/shard_map/pallas_call | solution.py:37
  140.2 2.0 %all-to-all-done.5.parts_ref = f32[8,8,128]{2,1,0:T(8,128)S(1)} async-done(((f32[8,8,128]{2,1,0:T(8,128)}), f32[8,8,128]{2,1,0:T(8,128)S(1)}, u32[]{:S(2)}, u32[]{:S(2)}) %all-to-all-start.5) | async-done | bytes 32800 | tf_op jit(solution)/shard_map/all_to_all | solution.py:195
  142.1 0.9 shard_map.73
  (12 shorter events, 0.1 us)
Async XLA Ops:
  1.7 10.0 %collective-permute-start.1 = (f32[4,2,48,128]{3,2,1,0:T(8,128)S(1)}, f32[4,2,48,128]{3,2,1,0:T(8,128)S(1)}, u32[]{:S(2)}, u32[]{:S(2)}) collective-permute-start(f32[4,2,48,128]{3,2,1,0:T(8,128)S(1)} %get-tuple-element.43), channel_id=1, source_target_pairs={{1,0},{2,1},{3,2},{4,3},{5,4},{6,5},{7,6},{0,7},{9,8},{10,9},{11,1... | collective-permute-start | bytes 589832 | tf_op jit(solution)/shard_map/ppermute | solution.py:207
  6.7 8.8 %collective-permute-start = (f32[4,2,48,128]{3,2,1,0:T(8,128)S(1)}, f32[4,2,48,128]{3,2,1,0:T(8,128)S(1)}, u32[]{:S(2)}, u32[]{:S(2)}) collective-permute-start(f32[4,2,48,128]{3,2,1,0:T(8,128)S(1)} %get-tuple-element.44), channel_id=1, source_target_pairs={{0,1},{1,2},{2,3},{3,4},{4,5},{5,6},{6,7},{7,0},{8,9},{9,10},{10,1... | collective-permute-start | bytes 589832 | tf_op jit(solution)/shard_map/ppermute | solution.py:207
  6.7 1.3 copy-start
  8.0 1.0 copy-start.2
  9.0 0.9 copy-start.3
  9.8 0.7 copy-start.5
  68.7 14.5 %collective-permute-start.2 = (f32[12,2,48,128]{3,2,1,0:T(8,128)S(1)}, f32[12,2,48,128]{3,2,1,0:T(8,128)S(1)}, u32[]{:S(2)}, u32[]{:S(2)}) collective-permute-start(f32[12,2,48,128]{3,2,1,0:T(8,128)S(1)} %get-tuple-element.32), channel_id=1, source_target_pairs={{0,1},{1,0},{2,3},{3,2},{4,5},{5,4},{6,7},{7,6},{8,9},{9,8},{10,11... | collective-permute-start | bytes 1769480 | tf_op jit(solution)/shard_map/ppermute | solution.py:254
  96.7 14.6 %collective-permute-start.3 = (f32[12,2,48,128]{3,2,1,0:T(8,128)S(1)}, f32[12,2,48,128]{3,2,1,0:T(8,128)S(1)}, u32[]{:S(2)}, u32[]{:S(2)}) collective-permute-start(f32[12,2,48,128]{3,2,1,0:T(8,128)S(1)} %get-tuple-element.39), channel_id=1, source_target_pairs={{0,1},{1,0},{2,3},{3,2},{4,5},{5,4},{6,7},{7,6},{8,9},{9,8},{10,11... | collective-permute-start | bytes 1769480 | tf_op jit(solution)/shard_map/ppermute | solution.py:259
  110.2 26.9 %copy-start.1 = (f32[12,4,48,128]{3,2,1,0:T(8,128)S(1)}, f32[12,4,48,128]{3,2,1,0:T(8,128)}, u32[]{:S(2)}) copy-start(f32[12,4,48,128]{3,2,1,0:T(8,128)} %field_ref.3) | copy-start | bytes 3538948
  110.2 26.9 %copy-start.4 = (f32[4,48,128]{2,1,0:T(8,128)S(1)}, f32[4,48,128]{2,1,0:T(8,128)}, u32[]{:S(2)}) copy-start(f32[4,48,128]{2,1,0:T(8,128)} %pot_ref.3) | copy-start | bytes 294916
  111.4 21.5 %all-to-all-start.4 = ((f32[32,24,128]{2,1,0:T(8,128)}), f32[32,24,128]{2,1,0:T(8,128)S(1)}, u32[]{:S(2)}, u32[]{:S(2)}) async-start(f32[32,24,128]{2,1,0:T(8,128)} %bitcast.2), calls=%async_computation.4 | async-start | bytes 786432 | tf_op jit(solution)/shard_map/all_to_all | solution.py:195
  117.5 19.5 %collective-permute-start.4 = (f32[12,2,48,128]{3,2,1,0:T(8,128)S(1)}, f32[12,2,48,128]{3,2,1,0:T(8,128)S(1)}, u32[]{:S(2)}, u32[]{:S(2)}) collective-permute-start(f32[12,2,48,128]{3,2,1,0:T(8,128)S(1)} %collective-permute-done.3), channel_id=1, source_target_pairs={{0,2},{1,7},{2,4},{3,1},{4,6},{5,3},{6,0},{7,5},{8,10},{9,15},{10,... | collective-permute-start | bytes 1769480 | tf_op jit(solution)/shard_map/ppermute | solution.py:270
  133.6 8.6 %all-to-all-start.5 = ((f32[8,8,128]{2,1,0:T(8,128)}), f32[8,8,128]{2,1,0:T(8,128)S(1)}, u32[]{:S(2)}, u32[]{:S(2)}) async-start(f32[8,8,128]{2,1,0:T(8,128)} %broadcast_in_dim.8), calls=%async_computation.5 | async-start | bytes 65536 | tf_op jit(solution)/shard_map/all_to_all | solution.py:195

commit v4 on v3

--- a/solution.py
+++ b/solution.py
@@ -23,14 +23,17 @@
 PARAMS = pltpu.CompilerParams(vmem_limit_bytes=16 * 1024 * 1024)
 
 
-def call(kernel, out_shape, in_specs, flops, nbytes):
+def call(kernel, out_shape, in_specs, flops, nbytes, pin=False, scratch=()):
     single = isinstance(out_shape[0], int)
     shapes = [out_shape] if single else list(out_shape)
     outs = pl.pallas_call(
         kernel,
-        out_shape=[jax.ShapeDtypeStruct(s, jnp.float32) for s in shapes],
+        out_shape=[
+            pltpu.VMEM(s, jnp.float32) if pin else jax.ShapeDtypeStruct(s, jnp.float32) for s in shapes
+        ],
         in_specs=in_specs,
         out_specs=[VMEM] * len(shapes),
+        scratch_shapes=[pltpu.VMEM(s, jnp.float32) for s in scratch],
         compiler_params=PARAMS,
         cost_estimate=pl.CostEstimate(flops=flops, bytes_accessed=nbytes, transcendentals=0),
     )
@@ -124,13 +127,16 @@
             put(packed_ref, nprior + n, z, field_ref[n, z] - step * value, nz)
 
 
+def split_cells(cells_ref, prior_ref, trial_ref):
+    count, split = prior_ref.shape[0] // NORB, trial_ref.shape[0] // NORB
+    for s in range(NORB):
+        prior_ref[s * count : (s + 1) * count, :] = cells_ref[s, :count, :]
+        trial_ref[s * split : (s + 1) * split, :] = cells_ref[s, count:, :]
+
+
 def make_coef_kernel(nprior, nblk, rows):
-    count, split = nprior // NORB * rows, nblk // NORB * rows
-
     def kernel(cells_ref, out_ref, prior_ref, trial_ref):
-        for s in range(NORB):
-            prior_ref[s * count : (s + 1) * count, :] = cells_ref[s, :count, :]
-            trial_ref[s * split : (s + 1) * split, :] = cells_ref[s, count:, :]
+        split_cells(cells_ref, prior_ref, trial_ref)
         total = jnp.zeros((nprior, nblk), jnp.float32)
         for r in range(rows):
             left = prior_ref[pl.ds(r, nprior, stride=rows), :]
@@ -145,7 +151,8 @@
 
 
 def make_proj_kernel(nprior, nblk, rows):
-    def kernel(coef_ref, prior_ref, trial_ref, out_ref):
+    def kernel(coef_ref, cells_ref, out_ref, prior_ref, trial_ref):
+        split_cells(cells_ref, prior_ref, trial_ref)
         coef_t = coef_ref[...].T
         for r in range(rows):
             left = prior_ref[pl.ds(r, nprior, stride=rows), :]
@@ -167,9 +174,13 @@
     for s in range(1, proj_ref.shape[0]):
         value = proj_ref[s]
         total = total + value * value
-    out_ref[...] = jnp.zeros_like(out_ref)
-    for n in range(count):
-        out_ref[n : n + 1, :] = jnp.sum(total[n * rows : (n + 1) * rows], axis=0, keepdims=True)
+    zero = jnp.zeros((out_ref.shape[1] - count, LANES), jnp.float32)
+    sums = [
+        jnp.sum(total[n * rows : (n + 1) * rows], axis=0, keepdims=True) for n in range(count)
+    ]
+    sums = jnp.concatenate(sums + [zero], axis=0)
+    for s in range(out_ref.shape[0]):
+        out_ref[s] = sums
 
 
 def make_scale_kernel(ncells):
@@ -240,7 +251,19 @@
     )(prior_rows, field, inner, steps, blow, bhigh)
     moved = exchange(packed, ORB)
 
-    moved, near, wrapped = lax.optimization_barrier((moved, near, wrapped))
+    moved, wrapped = lax.optimization_barrier((moved, wrapped))
+    coef_bytes = 4 * nprior * nblk
+    gemm = 2 * nprior * nblk * rows * LANES
+    apart = [(nprior * rows, LANES), (nblk * rows, LANES)]
+    partial = call(
+        make_coef_kernel(nprior, nblk, rows),
+        (nprior, nblk),
+        [VMEM],
+        gemm,
+        8 * coef_bytes,
+        scratch=apart,
+    )(moved)
+    moved, wrapped = lax.optimization_barrier((moved, wrapped))
     coef_bytes = 4 * nprior * nblk
     gemm = 2 * nprior * nblk * rows * LANES
     partial, prior_cells, trial_cells = call(
@@ -262,18 +285,21 @@
     proj = call(
         make_proj_kernel(nprior, nblk, rows),
         (nblk * rows, LANES),
-        [VMEM] * 3,
+        [VMEM] * 2,
         gemm,
-        6 * coef_bytes,
-    )(coeff, prior_cells, trial_cells)
+        10 * coef_bytes,
+        scratch=apart,
+    )(coeff, moved)
     proj, wrapped = lax.optimization_barrier((proj, wrapped))
     wrapped = lax.ppermute(wrapped, GRID, ALONG)
     back = exchange(proj.reshape(NORB, nblk_loc * rows, LANES), ORB)
     hprior = call(
         prior_kernel, prior.shape, [VMEM] * 4, 20 * nprior_loc * cells, 3 * nprior_loc * size
     )(prior, near, wrapped, potential)
-    squares = call(square_kernel, (8, LANES), [VMEM], 2 * nblk_loc * cells, nblk_loc * size)(back)
-    totals = exchange(repeat(squares, NGRID), GRID)
+    squares = call(
+        square_kernel, (NGRID, 8, LANES), [VMEM], 2 * nblk_loc * cells, nblk_loc * size, pin=True
+    )(back)
+    totals = exchange(squares, GRID)
     ortho = call(
         make_scale_kernel(ncells),
         (nblk_loc, nz * nx, ny),

time: 144 us -> 142 us (0.986)
  blocking collectives: 85.5 us -> 33.7 us
  waiting for transfers between devices: 24.7 us -> 61.9 us
  starting transfers between devices: 17.2 us -> 29.6 us
    all_to_all x4 -> x3, blocking collectives: 85.5 us -> 33.7 us  [exchange(): return lax.all_to_all(value, axes, 0, 0, tiled=True)]
    all_to_all x2 -> x3, waiting for transfers between devices: 17.2 us -> 57.3 us  [exchange(): return lax.all_to_all(value, axes, 0, 0, tiled=True)]
    all_to_all x2 -> x3, starting transfers between devices: 9.64 us -> 22.2 us  [exchange(): return lax.all_to_all(value, axes, 0, 0, tiled=True)]
    ppermute x1, waiting for transfers between devices: 2.44 us -> 0.01 us  [on_device(): near = lax.ppermute(near, 'zl', SWAP)]
  transfers between devices with their start and end apart: 7 -> 8, of which waited for: 5 -> 5; matrix products, arithmetic and copies ran while one was open for 0% -> 0% of each run, Pallas kernels for 5% -> 6%
where the time goes in v4:
time: 142 us; the launch traced here: 141 us
  waiting for transfers between devices  61.9 us (44%)
  blocking collectives  33.7 us (24%)
  starting transfers between devices  29.6 us (21%)
  Pallas kernels  10.6 us (7%)
  local copies, waits for them, and re-layouts  4.9 us (3%)
    all_to_all x3, waiting for transfers between devices, exchange(): return lax.all_to_all(value, axes, 0, 0, tiled=True)  57.3 us
    all_to_all x3, blocking collectives, exchange(): return lax.all_to_all(value, axes, 0, 0, tiled=True)  33.7 us
    all_to_all x3, starting transfers between devices, exchange(): return lax.all_to_all(value, axes, 0, 0, tiled=True)  22.2 us
    pallas_call x4, Pallas kernels, call(): return (lambda *a: outs(*a)[0]) if single else outs  6.57 us
    ppermute x1, starting transfers between devices, halos(): lax.ppermute(sides[1], GRID, BACKWARD)  4.99 us
    ppermute x1, waiting for transfers between devices, halos(): lax.ppermute(sides[0], GRID, FORWARD)  3.82 us
    unnamed x12, local copies, waits for them, and re-layouts  3.82 us
  transfers between devices with their start and end apart: 8, of which 5 were waited for; matrix products, arithmetic and copies ran while one was open for 0% of the time, Pallas kernels for 6%

profile of v4, /device:TPU:1, one launch (start us, length us, event | category | flops | bytes accessed | tf_op | source)
XLA Modules:
  0.0 141.5 jit_solution(9023280518796991632)
XLA Ops:
  0.6 1.1 fusion
  1.7 5.0 %collective-permute-start.1 = (f32[4,2,48,128]{3,2,1,0:T(8,128)S(1)}, f32[4,2,48,128]{3,2,1,0:T(8,128)S(1)}, u32[]{:S(2)}, u32[]{:S(2)}) collective-permute-start(f32[4,2,48,128]{3,2,1,0:T(8,128)S(1)} %get-tuple-element.37), channel_id=1, source_target_pairs={{1,0},{2,1},{3,2},{4,3},{5,4},{6,5},{7,6},{0,7},{9,8},{10,9},{11,1... | collective-permute-start | bytes 589832 | tf_op jit(solution)/shard_map/ppermute | solution.py:218
  6.7 0.0 collective-permute-start
  6.7 1.3 copy-done
  8.0 1.0 copy-done.2
  9.0 0.9 copy-done.3
  9.8 0.7 copy-done.5
  10.5 1.2 shard_map.67
  11.7 0.0 collective-permute-done.1.high_ref
  11.7 3.8 %collective-permute-done.low_ref = f32[4,2,48,128]{3,2,1,0:T(8,128)S(1)} collective-permute-done((f32[4,2,48,128]{3,2,1,0:T(8,128)S(1)}, f32[4,2,48,128]{3,2,1,0:T(8,128)S(1)}, u32[]{:S(2)}, u32[]{:S(2)}) %collective-permute-start) | collective-permute-done | bytes 196640 | tf_op jit(solution)/shard_map/ppermute | solution.py:218
  15.5 1.5 %shard_map.68 = (f32[4,4,48,128]{3,2,1,0:T(8,128)}, f32[32,96,128]{2,1,0:T(8,128)}) custom-call(f32[32,72,128]{2,1,0:T(8,128)S(1)} %get-tuple-element.20.prior_ref, f32[4,4,48,128]{3,2,1,0:T(8,128)S(1)} %get-tuple-element.21.field_ref, f32[4,4,48,128]{3,2,1,0:T(8,128)S(1)} %get-tuple-element.22.inner_ref, f32[4,8,128]{2,1,0:T(8,128)S(1)} %get-tuple-element.23.steps_ref, ...), custom_call_target="tpu_custom_call" | custom-call | flops 393216 | bytes 3932160 | tf_op jit(solution)/shard_map/pallas_call | solution.py:245
  17.0 12.1 %all-to-all-start = ((f32[32,96,128]{2,1,0:T(8,128)}), f32[32,96,128]{2,1,0:T(8,128)S(1)}, u32[]{:S(2)}, u32[]{:S(2)}) async-start(f32[32,96,128]{2,1,0:T(8,128)} %get-tuple-element.24), calls=%async_computation | async-start | bytes 3145728 | tf_op jit(solution)/shard_map/all_to_all | solution.py:206
  29.1 0.8 collective-permute-start.2
  30.0 40.0 %all-to-all-done.cells_ref = f32[32,96,128]{2,1,0:T(8,128)S(1)} async-done(((f32[32,96,128]{2,1,0:T(8,128)}), f32[32,96,128]{2,1,0:T(8,128)S(1)}, u32[]{:S(2)}, u32[]{:S(2)}) %all-to-all-start) | async-done | bytes 1572896 | tf_op jit(solution)/shard_map/all_to_all | solution.py:206
  69.9 1.3 shard_map.69
  71.3 9.7 %all_to_all.30 = f32[16,24,128]{2,1,0:T(8,128)S(1)} all-to-all(f32[16,24,128]{2,1,0:T(8,128)S(1)} %bitcast.5), channel_id=1, replica_groups=mesh['x'=4,'zh'=4,'core'=2,'y'=4,'zl'=2] {'x','y'}, dimensions={0} | all-to-all | bytes 393216 | tf_op jit(solution)/shard_map/all_to_all | solution.py:206
  81.0 0.0 collective-permute-done.2.near_ref
  81.0 13.7 %all_to_all.31 = f32[16,24,128]{2,1,0:T(8,128)S(1)} all-to-all(f32[16,24,128]{2,1,0:T(8,128)S(1)} %broadcast_in_dim.4), channel_id=1, replica_groups=mesh['x'=4,'zh'=4,'core'=2,'y'=4,'zl'=2] {'zh','core','zl'}, dimensions={0} | all-to-all | bytes 393216 | tf_op jit(solution)/shard_map/all_to_all | solution.py:206
  94.7 1.5 %collective-permute-start.3 = (f32[12,2,48,128]{3,2,1,0:T(8,128)S(1)}, f32[12,2,48,128]{3,2,1,0:T(8,128)S(1)}, u32[]{:S(2)}, u32[]{:S(2)}) collective-permute-start(f32[12,2,48,128]{3,2,1,0:T(8,128)S(1)} %get-tuple-element.33), channel_id=1, source_target_pairs={{0,1},{1,0},{2,3},{3,2},{4,5},{5,4},{6,7},{7,6},{8,9},{9,8},{10,11... | collective-permute-start | bytes 1769480 | tf_op jit(solution)/shard_map/ppermute | solution.py:282
  96.2 10.4 %all_to_all.32 = f32[16,24,128]{2,1,0:T(8,128)S(1)} all-to-all(f32[16,24,128]{2,1,0:T(8,128)S(1)} %broadcast_in_dim.5), channel_id=1, replica_groups=mesh['x'=4,'zh'=4,'core'=2,'y'=4,'zl'=2] {'x','y'}, dimensions={0} | all-to-all | bytes 393216 | tf_op jit(solution)/shard_map/all_to_all | solution.py:206
  106.6 1.9 %shard_map.70 = f32[768,128]{1,0:T(8,128)} custom-call(f32[384,128]{1,0:T(8,128)S(1)} %bitcast.4, f32[32,96,128]{2,1,0:T(8,128)S(1)} %all-to-all-done.cells_ref), custom_call_target="tpu_custom_call" | custom-call | flops 75497472 | bytes 1966080 | tf_op jit(solution)/shard_map/pallas_call | solution.py:40
  108.5 0.8 collective-permute-done.3
  109.3 5.9 %all-to-all-start.4 = ((f32[32,24,128]{2,1,0:T(8,128)}), f32[32,24,128]{2,1,0:T(8,128)S(1)}, u32[]{:S(2)}, u32[]{:S(2)}) async-start(f32[32,24,128]{2,1,0:T(8,128)} %bitcast.2), calls=%async_computation.4 | async-start | bytes 786432 | tf_op jit(solution)/shard_map/all_to_all | solution.py:206
  115.2 0.1 collective-permute-start.4
  115.3 15.3 %all-to-all-done.4.proj_ref = f32[32,24,128]{2,1,0:T(8,128)S(1)} async-done(((f32[32,24,128]{2,1,0:T(8,128)}), f32[32,24,128]{2,1,0:T(8,128)S(1)}, u32[]{:S(2)}, u32[]{:S(2)}) %all-to-all-start.4) | async-done | bytes 393248 | tf_op jit(solution)/shard_map/all_to_all | solution.py:206
  130.6 0.7 shard_map.72
  131.3 4.2 %all-to-all-start.5 = ((f32[8,8,128]{2,1,0:T(8,128)}), f32[8,8,128]{2,1,0:T(8,128)S(1)}, u32[]{:S(2)}, u32[]{:S(2)}) async-start(f32[8,8,128]{2,1,0:T(8,128)} %shard_map.72), calls=%async_computation.5 | async-start | bytes 65536 | tf_op jit(solution)/shard_map/all_to_all | solution.py:206
  135.4 0.0 collective-permute-done.4.wrapped_ref
  135.5 0.0 copy-done.1
  135.5 3.1 %shard_map.71 = f32[12,4,48,128]{3,2,1,0:T(8,128)} custom-call(f32[12,4,48,128]{3,2,1,0:T(8,128)S(1)} %copy-done.1, f32[12,2,48,128]{3,2,1,0:T(8,128)S(1)} %collective-permute-done.2.near_ref, f32[12,2,48,128]{3,2,1,0:T(8,128)S(1)} %collective-permute-done.4.wrapped_ref, f32[4,48,128]{2,1,0:T(8,128)S(1)} %copy-done.4), custom_call_target="tpu_custom_call" | custom-call | flops 5898240 | bytes 3538944 | tf_op jit(solution)/shard_map/pallas_call | solution.py:40
  138.6 2.0 %all-to-all-done.5.parts_ref = f32[8,8,128]{2,1,0:T(8,128)S(1)} async-done(((f32[8,8,128]{2,1,0:T(8,128)}), f32[8,8,128]{2,1,0:T(8,128)S(1)}, u32[]{:S(2)}, u32[]{:S(2)}) %all-to-all-start.5) | async-done | bytes 32800 | tf_op jit(solution)/shard_map/all_to_all | solution.py:206
  140.6 0.9 shard_map.73
  (12 shorter events, 0.1 us)
Async XLA Ops:
  1.7 10.0 %collective-permute-start.1 = (f32[4,2,48,128]{3,2,1,0:T(8,128)S(1)}, f32[4,2,48,128]{3,2,1,0:T(8,128)S(1)}, u32[]{:S(2)}, u32[]{:S(2)}) collective-permute-start(f32[4,2,48,128]{3,2,1,0:T(8,128)S(1)} %get-tuple-element.37), channel_id=1, source_target_pairs={{1,0},{2,1},{3,2},{4,3},{5,4},{6,5},{7,6},{0,7},{9,8},{10,9},{11,1... | collective-permute-start | bytes 589832 | tf_op jit(solution)/shard_map/ppermute | solution.py:218
  6.7 8.8 %collective-permute-start = (f32[4,2,48,128]{3,2,1,0:T(8,128)S(1)}, f32[4,2,48,128]{3,2,1,0:T(8,128)S(1)}, u32[]{:S(2)}, u32[]{:S(2)}) collective-permute-start(f32[4,2,48,128]{3,2,1,0:T(8,128)S(1)} %get-tuple-element.38), channel_id=1, source_target_pairs={{0,1},{1,2},{2,3},{3,4},{4,5},{5,6},{6,7},{7,0},{8,9},{9,10},{10,1... | collective-permute-start | bytes 589832 | tf_op jit(solution)/shard_map/ppermute | solution.py:218
  6.7 1.3 copy-start
  8.0 1.0 copy-start.2
  9.0 0.9 copy-start.3
  9.8 0.7 copy-start.5
  17.0 52.9 %all-to-all-start = ((f32[32,96,128]{2,1,0:T(8,128)}), f32[32,96,128]{2,1,0:T(8,128)S(1)}, u32[]{:S(2)}, u32[]{:S(2)}) async-start(f32[32,96,128]{2,1,0:T(8,128)} %get-tuple-element.24), calls=%async_computation | async-start | bytes 3145728 | tf_op jit(solution)/shard_map/all_to_all | solution.py:206
  29.1 51.9 %collective-permute-start.2 = (f32[12,2,48,128]{3,2,1,0:T(8,128)S(1)}, f32[12,2,48,128]{3,2,1,0:T(8,128)S(1)}, u32[]{:S(2)}, u32[]{:S(2)}) collective-permute-start(f32[12,2,48,128]{3,2,1,0:T(8,128)S(1)} %get-tuple-element.28), channel_id=1, source_target_pairs={{0,1},{1,0},{2,3},{3,2},{4,5},{5,4},{6,7},{7,6},{8,9},{9,8},{10,11... | collective-permute-start | bytes 1769480 | tf_op jit(solution)/shard_map/ppermute | solution.py:277
  94.7 14.6 %collective-permute-start.3 = (f32[12,2,48,128]{3,2,1,0:T(8,128)S(1)}, f32[12,2,48,128]{3,2,1,0:T(8,128)S(1)}, u32[]{:S(2)}, u32[]{:S(2)}) collective-permute-start(f32[12,2,48,128]{3,2,1,0:T(8,128)S(1)} %get-tuple-element.33), channel_id=1, source_target_pairs={{0,1},{1,0},{2,3},{3,2},{4,5},{5,4},{6,7},{7,6},{8,9},{9,8},{10,11... | collective-permute-start | bytes 1769480 | tf_op jit(solution)/shard_map/ppermute | solution.py:282
  108.5 26.9 %copy-start.1 = (f32[12,4,48,128]{3,2,1,0:T(8,128)S(1)}, f32[12,4,48,128]{3,2,1,0:T(8,128)}, u32[]{:S(2)}) copy-start(f32[12,4,48,128]{3,2,1,0:T(8,128)} %field_ref.3) | copy-start | bytes 3538948
  108.5 27.0 %copy-start.4 = (f32[4,48,128]{2,1,0:T(8,128)S(1)}, f32[4,48,128]{2,1,0:T(8,128)}, u32[]{:S(2)}) copy-start(f32[4,48,128]{2,1,0:T(8,128)} %pot_ref.3) | copy-start | bytes 294916
  109.3 21.3 %all-to-all-start.4 = ((f32[32,24,128]{2,1,0:T(8,128)}), f32[32,24,128]{2,1,0:T(8,128)S(1)}, u32[]{:S(2)}, u32[]{:S(2)}) async-start(f32[32,24,128]{2,1,0:T(8,128)} %bitcast.2), calls=%async_computation.4 | async-start | bytes 786432 | tf_op jit(solution)/shard_map/all_to_all | solution.py:206
  115.2 20.2 %collective-permute-start.4 = (f32[12,2,48,128]{3,2,1,0:T(8,128)S(1)}, f32[12,2,48,128]{3,2,1,0:T(8,128)S(1)}, u32[]{:S(2)}, u32[]{:S(2)}) collective-permute-start(f32[12,2,48,128]{3,2,1,0:T(8,128)S(1)} %collective-permute-done.3), channel_id=1, source_target_pairs={{0,2},{1,7},{2,4},{3,1},{4,6},{5,3},{6,0},{7,5},{8,10},{9,15},{10,... | collective-permute-start | bytes 1769480 | tf_op jit(solution)/shard_map/ppermute | solution.py:294
  131.3 9.3 %all-to-all-start.5 = ((f32[8,8,128]{2,1,0:T(8,128)}), f32[8,8,128]{2,1,0:T(8,128)S(1)}, u32[]{:S(2)}, u32[]{:S(2)}) async-start(f32[8,8,128]{2,1,0:T(8,128)} %shard_map.72), calls=%async_computation.5 | async-start | bytes 65536 | tf_op jit(solution)/shard_map/all_to_all | solution.py:206

commit v5 on v4

--- a/solution.py
+++ b/solution.py
@@ -154,14 +154,19 @@
     def kernel(coef_ref, cells_ref, out_ref, prior_ref, trial_ref):
         split_cells(cells_ref, prior_ref, trial_ref)
         coef_t = coef_ref[...].T
-        for r in range(rows):
-            left = prior_ref[pl.ds(r, nprior, stride=rows), :]
+        for r in range(0, rows, 2):
+            pair = [prior_ref[pl.ds(r + k, nprior, stride=rows), :] for k in range(2)]
             removed = jnp.dot(
-                coef_t, left, precision=HIGHEST, preferred_element_type=jnp.float32
+                coef_t,
+                jnp.concatenate(pair, axis=1),
+                precision=HIGHEST,
+                preferred_element_type=jnp.float32,
             )
-            out_ref[pl.ds(r, nblk, stride=rows), :] = (
-                trial_ref[pl.ds(r, nblk, stride=rows), :] - removed
-            )
+            for k in range(2):
+                out_ref[pl.ds(r + k, nblk, stride=rows), :] = (
+                    trial_ref[pl.ds(r + k, nblk, stride=rows), :]
+                    - removed[:, k * LANES : (k + 1) * LANES]
+                )
 
     return kernel
 
@@ -276,10 +281,9 @@
     first = 16
     near = lax.ppermute(near, "zl", SWAP)
     share = jnp.sum(exchange(partial.reshape(first, nprior // first, nblk), ("x", "y")), axis=0)
-    share, near = lax.optimization_barrier((share, near))
+    share, near, wrapped = lax.optimization_barrier((share, near, wrapped))
+    wrapped = lax.ppermute(wrapped, "zl", SWAP)
     share = jnp.sum(exchange(repeat(share, 16), ("zh", "core", "zl")), axis=0) / ncells
-    share, wrapped = lax.optimization_barrier((share, wrapped))
-    wrapped = lax.ppermute(wrapped, "zl", SWAP)
     coeff = exchange(repeat(share, first), ("x", "y")).reshape(nprior, nblk)
 
     proj = call(

time: 142 us -> 142 us (level)
  blocking collectives: 33.7 us -> 19.9 us
  waiting for transfers between devices: 61.9 us -> 68.4 us
  starting transfers between devices: 29.6 us -> 36 us
    all_to_all x3 -> x2, blocking collectives: 33.7 us -> 19.9 us  [exchange(): return lax.all_to_all(value, axes, 0, 0, tiled=True)]
    all_to_all x3 -> x4, waiting for transfers between devices: 57.3 us -> 64.5 us  [exchange(): return lax.all_to_all(value, axes, 0, 0, tiled=True)]
    all_to_all x3 -> x4, starting transfers between devices: 22.2 us -> 28.5 us  [exchange(): return lax.all_to_all(value, axes, 0, 0, tiled=True)]
  transfers between devices with their start and end apart: 8 -> 9, of which waited for: 5 -> 5; matrix products, arithmetic and copies ran while one was open for 0% -> 0% of each run, Pallas kernels for 6% -> 6%
where the time goes in v5:
time: 142 us; the launch traced here: 141 us
  waiting for transfers between devices  68.4 us (48%)
  starting transfers between devices  36 us (25%)
  blocking collectives  19.9 us (14%)
  Pallas kernels  10.3 us (7%)
  local copies, waits for them, and re-layouts  5.58 us (4%)
    all_to_all x4, waiting for transfers between devices, exchange(): return lax.all_to_all(value, axes, 0, 0, tiled=True)  64.5 us
    all_to_all x4, starting transfers between devices, exchange(): return lax.all_to_all(value, axes, 0, 0, tiled=True)  28.5 us
    all_to_all x2, blocking collectives, exchange(): return lax.all_to_all(value, axes, 0, 0, tiled=True)  19.9 us
    pallas_call x4, Pallas kernels, call(): return (lambda *a: outs(*a)[0]) if single else outs  6.3 us
    ppermute x1, starting transfers between devices, halos(): lax.ppermute(sides[1], GRID, BACKWARD)  4.99 us
    ppermute x1, waiting for transfers between devices, halos(): lax.ppermute(sides[0], GRID, FORWARD)  3.82 us
    unnamed x12, local copies, waits for them, and re-layouts  3.82 us
  transfers between devices with their start and end apart: 9, of which 5 were waited for; matrix products, arithmetic and copies ran while one was open for 0% of the time, Pallas kernels for 6%

profile of v5, /device:TPU:1, one launch (start us, length us, event | category | flops | bytes accessed | tf_op | source)
XLA Modules:
  0.0 140.9 jit_solution(16151069469671681917)
XLA Ops:
  0.6 1.1 fusion
  1.7 5.0 %collective-permute-start.1 = (f32[4,2,48,128]{3,2,1,0:T(8,128)S(1)}, f32[4,2,48,128]{3,2,1,0:T(8,128)S(1)}, u32[]{:S(2)}, u32[]{:S(2)}) collective-permute-start(f32[4,2,48,128]{3,2,1,0:T(8,128)S(1)} %get-tuple-element.35), channel_id=1, source_target_pairs={{1,0},{2,1},{3,2},{4,3},{5,4},{6,5},{7,6},{0,7},{9,8},{10,9},{11,1... | collective-permute-start | bytes 589832 | tf_op jit(solution)/shard_map/ppermute | solution.py:223
  6.7 0.0 collective-permute-start
  6.7 1.3 copy-done
  8.0 1.0 copy-done.2
  9.0 0.9 copy-done.3
  9.8 0.7 copy-done.5
  10.5 1.2 shard_map.67
  11.7 0.0 collective-permute-done.1.high_ref
  11.7 3.8 %collective-permute-done.low_ref = f32[4,2,48,128]{3,2,1,0:T(8,128)S(1)} collective-permute-done((f32[4,2,48,128]{3,2,1,0:T(8,128)S(1)}, f32[4,2,48,128]{3,2,1,0:T(8,128)S(1)}, u32[]{:S(2)}, u32[]{:S(2)}) %collective-permute-start) | collective-permute-done | bytes 196640 | tf_op jit(solution)/shard_map/ppermute | solution.py:223
  15.5 1.5 %shard_map.68 = (f32[4,4,48,128]{3,2,1,0:T(8,128)}, f32[32,96,128]{2,1,0:T(8,128)}) custom-call(f32[32,72,128]{2,1,0:T(8,128)S(1)} %get-tuple-element.19.prior_ref, f32[4,4,48,128]{3,2,1,0:T(8,128)S(1)} %get-tuple-element.20.field_ref, f32[4,4,48,128]{3,2,1,0:T(8,128)S(1)} %get-tuple-element.21.inner_ref, f32[4,8,128]{2,1,0:T(8,128)S(1)} %get-tuple-element.22.steps_ref, ...), custom_call_target="tpu_custom_call" | custom-call | flops 393216 | bytes 3932160 | tf_op jit(solution)/shard_map/pallas_call | solution.py:250
  17.0 12.1 %all-to-all-start = ((f32[32,96,128]{2,1,0:T(8,128)}), f32[32,96,128]{2,1,0:T(8,128)S(1)}, u32[]{:S(2)}, u32[]{:S(2)}) async-start(f32[32,96,128]{2,1,0:T(8,128)} %get-tuple-element.23), calls=%async_computation | async-start | bytes 3145728 | tf_op jit(solution)/shard_map/all_to_all | solution.py:211
  29.2 0.8 collective-permute-start.2
  30.0 40.0 %all-to-all-done.cells_ref = f32[32,96,128]{2,1,0:T(8,128)S(1)} async-done(((f32[32,96,128]{2,1,0:T(8,128)}), f32[32,96,128]{2,1,0:T(8,128)S(1)}, u32[]{:S(2)}, u32[]{:S(2)}) %all-to-all-start) | async-done | bytes 1572896 | tf_op jit(solution)/shard_map/all_to_all | solution.py:211
  70.0 1.3 shard_map.69
  71.3 9.7 %all_to_all.30 = f32[16,24,128]{2,1,0:T(8,128)S(1)} all-to-all(f32[16,24,128]{2,1,0:T(8,128)S(1)} %bitcast.5), channel_id=1, replica_groups=mesh['x'=4,'zh'=4,'core'=2,'y'=4,'zl'=2] {'x','y'}, dimensions={0} | all-to-all | bytes 393216 | tf_op jit(solution)/shard_map/all_to_all | solution.py:211
  81.0 0.0 collective-permute-done.2.near_ref
  81.0 0.7 broadcast_in_dim.4
  81.7 5.1 %all-to-all-start.2 = ((f32[16,24,128]{2,1,0:T(8,128)}), f32[16,24,128]{2,1,0:T(8,128)S(1)}, u32[]{:S(2)}, u32[]{:S(2)}) async-start(f32[16,24,128]{2,1,0:T(8,128)} %broadcast_in_dim.4), calls=%async_computation.2 | async-start | bytes 393216 | tf_op jit(solution)/shard_map/all_to_all | solution.py:211
  86.8 1.4 collective-permute-start.3
  88.2 7.6 %all-to-all-done.2 = f32[16,24,128]{2,1,0:T(8,128)S(1)} async-done(((f32[16,24,128]{2,1,0:T(8,128)}), f32[16,24,128]{2,1,0:T(8,128)S(1)}, u32[]{:S(2)}, u32[]{:S(2)}) %all-to-all-start.2) | async-done | bytes 196640 | tf_op jit(solution)/shard_map/all_to_all | solution.py:211
  95.8 10.2 %all_to_all.31 = f32[16,24,128]{2,1,0:T(8,128)S(1)} all-to-all(f32[16,24,128]{2,1,0:T(8,128)S(1)} %broadcast_in_dim.5), channel_id=1, replica_groups=mesh['x'=4,'zh'=4,'core'=2,'y'=4,'zl'=2] {'x','y'}, dimensions={0} | all-to-all | bytes 393216 | tf_op jit(solution)/shard_map/all_to_all | solution.py:211
  106.1 1.7 %shard_map.70 = f32[768,128]{1,0:T(8,128)} custom-call(f32[384,128]{1,0:T(8,128)S(1)} %bitcast.4, f32[32,96,128]{2,1,0:T(8,128)S(1)} %all-to-all-done.cells_ref), custom_call_target="tpu_custom_call" | custom-call | flops 75497472 | bytes 1966080 | tf_op jit(solution)/shard_map/pallas_call | solution.py:40
  107.7 6.9 %all-to-all-start.4 = ((f32[32,24,128]{2,1,0:T(8,128)}), f32[32,24,128]{2,1,0:T(8,128)S(1)}, u32[]{:S(2)}, u32[]{:S(2)}) async-start(f32[32,24,128]{2,1,0:T(8,128)} %bitcast.2), calls=%async_computation.4 | async-start | bytes 786432 | tf_op jit(solution)/shard_map/all_to_all | solution.py:211
  114.7 0.2 collective-permute-start.4
  114.9 15.0 %all-to-all-done.4.proj_ref = f32[32,24,128]{2,1,0:T(8,128)S(1)} async-done(((f32[32,24,128]{2,1,0:T(8,128)}), f32[32,24,128]{2,1,0:T(8,128)S(1)}, u32[]{:S(2)}, u32[]{:S(2)}) %all-to-all-start.4) | async-done | bytes 393248 | tf_op jit(solution)/shard_map/all_to_all | solution.py:211
  129.9 0.7 shard_map.72
  130.6 4.3 %all-to-all-start.5 = ((f32[8,8,128]{2,1,0:T(8,128)}), f32[8,8,128]{2,1,0:T(8,128)S(1)}, u32[]{:S(2)}, u32[]{:S(2)}) async-start(f32[8,8,128]{2,1,0:T(8,128)} %shard_map.72), calls=%async_computation.5 | async-start | bytes 65536 | tf_op jit(solution)/shard_map/all_to_all | solution.py:211
  134.9 0.0 collective-permute-done.4.wrapped_ref
  135.0 3.1 %shard_map.71 = f32[12,4,48,128]{3,2,1,0:T(8,128)} custom-call(f32[12,4,48,128]{3,2,1,0:T(8,128)S(1)} %copy-done.1, f32[12,2,48,128]{3,2,1,0:T(8,128)S(1)} %collective-permute-done.2.near_ref, f32[12,2,48,128]{3,2,1,0:T(8,128)S(1)} %collective-permute-done.4.wrapped_ref, f32[4,48,128]{2,1,0:T(8,128)S(1)} %copy-done.4), custom_call_target="tpu_custom_call" | custom-call | flops 5898240 | bytes 3538944 | tf_op jit(solution)/shard_map/pallas_call | solution.py:40
  138.1 2.0 %all-to-all-done.5.parts_ref = f32[8,8,128]{2,1,0:T(8,128)S(1)} async-done(((f32[8,8,128]{2,1,0:T(8,128)}), f32[8,8,128]{2,1,0:T(8,128)S(1)}, u32[]{:S(2)}, u32[]{:S(2)}) %all-to-all-start.5) | async-done | bytes 32800 | tf_op jit(solution)/shard_map/all_to_all | solution.py:211
  140.0 0.9 shard_map.73
  (13 shorter events, 0.1 us)
Async XLA Ops:
  1.7 10.0 %collective-permute-start.1 = (f32[4,2,48,128]{3,2,1,0:T(8,128)S(1)}, f32[4,2,48,128]{3,2,1,0:T(8,128)S(1)}, u32[]{:S(2)}, u32[]{:S(2)}) collective-permute-start(f32[4,2,48,128]{3,2,1,0:T(8,128)S(1)} %get-tuple-element.35), channel_id=1, source_target_pairs={{1,0},{2,1},{3,2},{4,3},{5,4},{6,5},{7,6},{0,7},{9,8},{10,9},{11,1... | collective-permute-start | bytes 589832 | tf_op jit(solution)/shard_map/ppermute | solution.py:223
  6.7 8.8 %collective-permute-start = (f32[4,2,48,128]{3,2,1,0:T(8,128)S(1)}, f32[4,2,48,128]{3,2,1,0:T(8,128)S(1)}, u32[]{:S(2)}, u32[]{:S(2)}) collective-permute-start(f32[4,2,48,128]{3,2,1,0:T(8,128)S(1)} %get-tuple-element.36), channel_id=1, source_target_pairs={{0,1},{1,2},{2,3},{3,4},{4,5},{5,6},{6,7},{7,0},{8,9},{9,10},{10,1... | collective-permute-start | bytes 589832 | tf_op jit(solution)/shard_map/ppermute | solution.py:223
  6.7 1.3 copy-start
  8.0 1.0 copy-start.2
  9.0 0.9 copy-start.3
  9.8 0.7 copy-start.5
  17.0 52.9 %all-to-all-start = ((f32[32,96,128]{2,1,0:T(8,128)}), f32[32,96,128]{2,1,0:T(8,128)S(1)}, u32[]{:S(2)}, u32[]{:S(2)}) async-start(f32[32,96,128]{2,1,0:T(8,128)} %get-tuple-element.23), calls=%async_computation | async-start | bytes 3145728 | tf_op jit(solution)/shard_map/all_to_all | solution.py:211
  29.2 51.9 %collective-permute-start.2 = (f32[12,2,48,128]{3,2,1,0:T(8,128)S(1)}, f32[12,2,48,128]{3,2,1,0:T(8,128)S(1)}, u32[]{:S(2)}, u32[]{:S(2)}) collective-permute-start(f32[12,2,48,128]{3,2,1,0:T(8,128)S(1)} %get-tuple-element.27), channel_id=1, source_target_pairs={{0,1},{1,0},{2,3},{3,2},{4,5},{5,4},{6,7},{7,6},{8,9},{9,8},{10,11... | collective-permute-start | bytes 1769480 | tf_op jit(solution)/shard_map/ppermute | solution.py:282
  81.7 14.1 %all-to-all-start.2 = ((f32[16,24,128]{2,1,0:T(8,128)}), f32[16,24,128]{2,1,0:T(8,128)S(1)}, u32[]{:S(2)}, u32[]{:S(2)}) async-start(f32[16,24,128]{2,1,0:T(8,128)} %broadcast_in_dim.4), calls=%async_computation.2 | async-start | bytes 393216 | tf_op jit(solution)/shard_map/all_to_all | solution.py:211
  86.8 20.9 %collective-permute-start.3 = (f32[12,2,48,128]{3,2,1,0:T(8,128)S(1)}, f32[12,2,48,128]{3,2,1,0:T(8,128)S(1)}, u32[]{:S(2)}, u32[]{:S(2)}) collective-permute-start(f32[12,2,48,128]{3,2,1,0:T(8,128)S(1)} %get-tuple-element.31), channel_id=1, source_target_pairs={{0,1},{1,0},{2,3},{3,2},{4,5},{5,4},{6,7},{7,6},{8,9},{9,8},{10,11... | collective-permute-start | bytes 1769480 | tf_op jit(solution)/shard_map/ppermute | solution.py:285
  107.7 27.2 %copy-start.1 = (f32[12,4,48,128]{3,2,1,0:T(8,128)S(1)}, f32[12,4,48,128]{3,2,1,0:T(8,128)}, u32[]{:S(2)}) copy-start(f32[12,4,48,128]{3,2,1,0:T(8,128)} %field_ref.3) | copy-start | bytes 3538948
  107.7 27.2 %copy-start.4 = (f32[4,48,128]{2,1,0:T(8,128)S(1)}, f32[4,48,128]{2,1,0:T(8,128)}, u32[]{:S(2)}) copy-start(f32[4,48,128]{2,1,0:T(8,128)} %pot_ref.3) | copy-start | bytes 294916
  107.7 22.2 %all-to-all-start.4 = ((f32[32,24,128]{2,1,0:T(8,128)}), f32[32,24,128]{2,1,0:T(8,128)S(1)}, u32[]{:S(2)}, u32[]{:S(2)}) async-start(f32[32,24,128]{2,1,0:T(8,128)} %bitcast.2), calls=%async_computation.4 | async-start | bytes 786432 | tf_op jit(solution)/shard_map/all_to_all | solution.py:211
  114.7 20.2 %collective-permute-start.4 = (f32[12,2,48,128]{3,2,1,0:T(8,128)S(1)}, f32[12,2,48,128]{3,2,1,0:T(8,128)S(1)}, u32[]{:S(2)}, u32[]{:S(2)}) collective-permute-start(f32[12,2,48,128]{3,2,1,0:T(8,128)S(1)} %collective-permute-done.3), channel_id=1, source_target_pairs={{0,2},{1,7},{2,4},{3,1},{4,6},{5,3},{6,0},{7,5},{8,10},{9,15},{10,... | collective-permute-start | bytes 1769480 | tf_op jit(solution)/shard_map/ppermute | solution.py:298
  130.6 9.4 %all-to-all-start.5 = ((f32[8,8,128]{2,1,0:T(8,128)}), f32[8,8,128]{2,1,0:T(8,128)S(1)}, u32[]{:S(2)}, u32[]{:S(2)}) async-start(f32[8,8,128]{2,1,0:T(8,128)} %shard_map.72), calls=%async_computation.5 | async-start | bytes 65536 | tf_op jit(solution)/shard_map/all_to_all | solution.py:211

commit v6 on v5

--- a/solution.py
+++ b/solution.py
@@ -107,12 +107,11 @@
         steps_ref[n] = jnp.full((8, LANES), step_ref[n], jnp.float32)
 
 
-def outer_kernel(prior_ref, field_ref, inner_ref, steps_ref, low_ref, high_ref, out_ref, packed_ref):
+def outer_kernel(
+    prior_ref, field_ref, inner_ref, steps_ref, low_ref, high_ref, out_ref, packed_ref, trial_ref, sem
+):
     nblk, nz, nx, _ = field_ref.shape
     rows = nz * nx // NORB
-    nprior = prior_ref.shape[1] // rows
-    for dest in range(NORB):
-        packed_ref[dest, : nprior * rows, :] = prior_ref[dest]
     for n in range(nblk):
         edge = {
             0: FAR * low_ref[n, 0] - NEAR * low_ref[n, 1],
@@ -124,7 +123,12 @@
         for z in range(nz):
             value = inner_ref[n, z] + edge[z]
             out_ref[n, z] = value
-            put(packed_ref, nprior + n, z, field_ref[n, z] - step * value, nz)
+            put(trial_ref, n, z, field_ref[n, z] - step * value, nz)
+    width = nblk * rows
+    start = packed_ref.shape[1] - width
+    copy = pltpu.make_async_copy(trial_ref, packed_ref.at[:, pl.ds(start, width), :], sem)
+    copy.start()
+    copy.wait()
 
 
 def split_cells(cells_ref, prior_ref, trial_ref):
@@ -236,7 +240,7 @@
     prior_rows, near, wrapped, field, inner, steps = call(
         inner_kernel,
         [
-            (NORB, nprior_loc * rows, LANES),
+            (NORB, (nprior_loc + nblk_loc) * rows, LANES),
             (nprior_loc, 2, nx, ny),
             (nprior_loc, 2, nx, ny),
             block.shape,
@@ -247,12 +251,24 @@
         20 * nblk_loc * cells,
         (2 * nprior_loc + 4 * nblk_loc) * size,
     )(prior, block, potential, step_len)
-    hblock, packed = call(
+    total_rows = (nprior_loc + nblk_loc) * rows
+    hblock, packed = pl.pallas_call(
         outer_kernel,
-        [block.shape, (NORB, (nprior_loc + nblk_loc) * rows, LANES)],
-        [VMEM] * 6,
-        4 * nblk_loc * cells,
-        (2 * nprior_loc + 4 * nblk_loc) * size,
+        out_shape=[
+            jax.ShapeDtypeStruct(block.shape, jnp.float32),
+            jax.ShapeDtypeStruct((NORB, total_rows, LANES), jnp.float32),
+        ],
+        in_specs=[pl.BlockSpec(memory_space=pl.ANY)] + [VMEM] * 5,
+        out_specs=[VMEM, pl.BlockSpec(memory_space=pl.ANY)],
+        scratch_shapes=[
+            pltpu.VMEM((NORB, nblk_loc * rows, LANES), jnp.float32),
+            pltpu.SemaphoreType.DMA,
+        ],
+        input_output_aliases={0: 1},
+        compiler_params=PARAMS,
+        cost_estimate=pl.CostEstimate(
+            flops=4 * nblk_loc * cells, bytes_accessed=5 * nblk_loc * size, transcendentals=0
+        ),
     )(prior_rows, field, inner, steps, blow, bhigh)
     moved = exchange(packed, ORB)
 

time: 142 us -> 142 us (level)
  Pallas kernels: 10.3 us -> 11.8 us
    pallas_call x2, Pallas kernels: 2.68 us -> 4.16 us  [the longest x1 2.54 us: on_device(): call(inner_kernel, [(NORB, (nprior_loc + nblk_loc) * rows, LANES), (nprio...]
  transfers between devices with their start and end apart: 9 -> 9, of which waited for: 5 -> 5; matrix products, arithmetic and copies ran while one was open for 0% -> 0% of each run, Pallas kernels for 6% -> 7%
where the time goes in v6:
time: 142 us; the launch traced here: 141 us
  waiting for transfers between devices  67 us (47%)
  starting transfers between devices  35.8 us (25%)
  blocking collectives  19.9 us (14%)
  Pallas kernels  11.8 us (8%)
  local copies, waits for them, and re-layouts  5.58 us (4%)
    all_to_all x4, waiting for transfers between devices, exchange(): return lax.all_to_all(value, axes, 0, 0, tiled=True)  64.5 us
    all_to_all x4, starting transfers between devices, exchange(): return lax.all_to_all(value, axes, 0, 0, tiled=True)  28.4 us
    all_to_all x2, blocking collectives, exchange(): return lax.all_to_all(value, axes, 0, 0, tiled=True)  19.9 us
    pallas_call x4, Pallas kernels, call(): return (lambda *a: outs(*a)[0]) if single else outs  6.3 us
    ppermute x1, starting transfers between devices, halos(): lax.ppermute(sides[1], GRID, BACKWARD)  4.99 us
    unnamed x12, local copies, waits for them, and re-layouts  3.82 us
  transfers between devices with their start and end apart: 9, of which 5 were waited for; matrix products, arithmetic and copies ran while one was open for 0% of the time, Pallas kernels for 7%

profile of v6, /device:TPU:1, one launch (start us, length us, event | category | flops | bytes accessed | tf_op | source)
XLA Modules:
  0.0 140.9 jit_solution(2073473774069758405)
XLA Ops:
  0.6 1.1 fusion
  1.7 5.0 %collective-permute-start.1 = (f32[4,2,48,128]{3,2,1,0:T(8,128)S(1)}, f32[4,2,48,128]{3,2,1,0:T(8,128)S(1)}, u32[]{:S(2)}, u32[]{:S(2)}) collective-permute-start(f32[4,2,48,128]{3,2,1,0:T(8,128)S(1)} %get-tuple-element.35), channel_id=1, source_target_pairs={{1,0},{2,1},{3,2},{4,3},{5,4},{6,5},{7,6},{0,7},{9,8},{10,9},{11,1... | collective-permute-start | bytes 589832 | tf_op jit(solution)/shard_map/ppermute | solution.py:227
  6.7 1.3 copy-done
  8.0 1.0 copy-done.2
  9.0 0.9 copy-done.3
  9.8 0.7 copy-done.5
  10.5 2.5 %shard_map.67 = (f32[32,96,128]{2,1,0:T(8,128)}, f32[12,2,48,128]{3,2,1,0:T(8,128)S(1)}, f32[12,2,48,128]{3,2,1,0:T(8,128)}, f32[4,4,48,128]{3,2,1,0:T(8,128)S(1...) custom-call(f32[12,4,48,128]{3,2,1,0:T(8,128)S(1)} %copy-done, f32[4,4,48,128]{3,2,1,0:T(8,128)S(1)} %copy-done.2, ...), custom_call_target="tpu_custom_call" | custom-call | flops 1966080 | bytes 3932160 | tf_op jit(solution)/shard_map/pallas_call | solution.py:240
  13.0 0.0 collective-permute-done.1.high_ref
  13.0 2.5 %collective-permute-done.low_ref = f32[4,2,48,128]{3,2,1,0:T(8,128)S(1)} collective-permute-done((f32[4,2,48,128]{3,2,1,0:T(8,128)S(1)}, f32[4,2,48,128]{3,2,1,0:T(8,128)S(1)}, u32[]{:S(2)}, u32[]{:S(2)}) %collective-permute-start) | collective-permute-done | bytes 196640 | tf_op jit(solution)/shard_map/ppermute | solution.py:227
  15.5 1.6 %shard_map.68 = (f32[4,4,48,128]{3,2,1,0:T(8,128)}, f32[32,96,128]{2,1,0:T(8,128)}) custom-call(f32[32,96,128]{2,1,0:T(8,128)} %get-tuple-element.19.prior_ref, f32[4,4,48,128]{3,2,1,0:T(8,128)S(1)} %get-tuple-element.20.field_ref, f32[4,4,48,128]{3,2,1,0:T(8,128)S(1)} %get-tuple-element.21.inner_ref, ...), custom_call_target="tpu_custom_call", output_to_operand_aliasing={{1}: (0, {})} | custom-call | flops 393216 | bytes 1966080 | tf_op jit(solution)/shard_map/pallas_call | solution.py:255
  17.2 12.1 %all-to-all-start = ((f32[32,96,128]{2,1,0:T(8,128)}), f32[32,96,128]{2,1,0:T(8,128)S(1)}, u32[]{:S(2)}, u32[]{:S(2)}) async-start(f32[32,96,128]{2,1,0:T(8,128)} %get-tuple-element.23), calls=%async_computation | async-start | bytes 3145728 | tf_op jit(solution)/shard_map/all_to_all | solution.py:215
  29.3 0.8 collective-permute-start.2
  30.1 40.0 %all-to-all-done.cells_ref = f32[32,96,128]{2,1,0:T(8,128)S(1)} async-done(((f32[32,96,128]{2,1,0:T(8,128)}), f32[32,96,128]{2,1,0:T(8,128)S(1)}, u32[]{:S(2)}, u32[]{:S(2)}) %all-to-all-start) | async-done | bytes 1572896 | tf_op jit(solution)/shard_map/all_to_all | solution.py:215
  70.1 1.3 shard_map.69
  71.4 9.7 %all_to_all.30 = f32[16,24,128]{2,1,0:T(8,128)S(1)} all-to-all(f32[16,24,128]{2,1,0:T(8,128)S(1)} %bitcast.5), channel_id=1, replica_groups=mesh['x'=4,'zh'=4,'core'=2,'y'=4,'zl'=2] {'x','y'}, dimensions={0} | all-to-all | bytes 393216 | tf_op jit(solution)/shard_map/all_to_all | solution.py:215
  81.2 0.0 collective-permute-done.2.near_ref
  81.2 0.7 broadcast_in_dim.4
  81.9 5.1 %all-to-all-start.2 = ((f32[16,24,128]{2,1,0:T(8,128)}), f32[16,24,128]{2,1,0:T(8,128)S(1)}, u32[]{:S(2)}, u32[]{:S(2)}) async-start(f32[16,24,128]{2,1,0:T(8,128)} %broadcast_in_dim.4), calls=%async_computation.2 | async-start | bytes 393216 | tf_op jit(solution)/shard_map/all_to_all | solution.py:215
  87.0 1.4 collective-permute-start.3
  88.4 7.6 %all-to-all-done.2 = f32[16,24,128]{2,1,0:T(8,128)S(1)} async-done(((f32[16,24,128]{2,1,0:T(8,128)}), f32[16,24,128]{2,1,0:T(8,128)S(1)}, u32[]{:S(2)}, u32[]{:S(2)}) %all-to-all-start.2) | async-done | bytes 196640 | tf_op jit(solution)/shard_map/all_to_all | solution.py:215
  96.0 10.2 %all_to_all.31 = f32[16,24,128]{2,1,0:T(8,128)S(1)} all-to-all(f32[16,24,128]{2,1,0:T(8,128)S(1)} %broadcast_in_dim.5), channel_id=1, replica_groups=mesh['x'=4,'zh'=4,'core'=2,'y'=4,'zl'=2] {'x','y'}, dimensions={0} | all-to-all | bytes 393216 | tf_op jit(solution)/shard_map/all_to_all | solution.py:215
  106.2 1.7 %shard_map.70 = f32[768,128]{1,0:T(8,128)} custom-call(f32[384,128]{1,0:T(8,128)S(1)} %bitcast.4, f32[32,96,128]{2,1,0:T(8,128)S(1)} %all-to-all-done.cells_ref), custom_call_target="tpu_custom_call" | custom-call | flops 75497472 | bytes 1966080 | tf_op jit(solution)/shard_map/pallas_call | solution.py:40
  107.9 0.0 collective-permute-done.3
  107.9 6.8 %all-to-all-start.4 = ((f32[32,24,128]{2,1,0:T(8,128)}), f32[32,24,128]{2,1,0:T(8,128)S(1)}, u32[]{:S(2)}, u32[]{:S(2)}) async-start(f32[32,24,128]{2,1,0:T(8,128)} %bitcast.2), calls=%async_computation.4 | async-start | bytes 786432 | tf_op jit(solution)/shard_map/all_to_all | solution.py:215
  114.7 0.2 collective-permute-start.4
  114.9 15.0 %all-to-all-done.4.proj_ref = f32[32,24,128]{2,1,0:T(8,128)S(1)} async-done(((f32[32,24,128]{2,1,0:T(8,128)}), f32[32,24,128]{2,1,0:T(8,128)S(1)}, u32[]{:S(2)}, u32[]{:S(2)}) %all-to-all-start.4) | async-done | bytes 393248 | tf_op jit(solution)/shard_map/all_to_all | solution.py:215
  130.0 0.7 shard_map.72
  130.6 4.3 %all-to-all-start.5 = ((f32[8,8,128]{2,1,0:T(8,128)}), f32[8,8,128]{2,1,0:T(8,128)S(1)}, u32[]{:S(2)}, u32[]{:S(2)}) async-start(f32[8,8,128]{2,1,0:T(8,128)} %shard_map.72), calls=%async_computation.5 | async-start | bytes 65536 | tf_op jit(solution)/shard_map/all_to_all | solution.py:215
  134.9 0.0 collective-permute-done.4.wrapped_ref
  135.0 3.1 %shard_map.71 = f32[12,4,48,128]{3,2,1,0:T(8,128)} custom-call(f32[12,4,48,128]{3,2,1,0:T(8,128)S(1)} %copy-done.1, f32[12,2,48,128]{3,2,1,0:T(8,128)S(1)} %collective-permute-done.2.near_ref, f32[12,2,48,128]{3,2,1,0:T(8,128)S(1)} %collective-permute-done.4.wrapped_ref, f32[4,48,128]{2,1,0:T(8,128)S(1)} %copy-done.4), custom_call_target="tpu_custom_call" | custom-call | flops 5898240 | bytes 3538944 | tf_op jit(solution)/shard_map/pallas_call | solution.py:40
  138.1 2.0 %all-to-all-done.5.parts_ref = f32[8,8,128]{2,1,0:T(8,128)S(1)} async-done(((f32[8,8,128]{2,1,0:T(8,128)}), f32[8,8,128]{2,1,0:T(8,128)S(1)}, u32[]{:S(2)}, u32[]{:S(2)}) %all-to-all-start.5) | async-done | bytes 32800 | tf_op jit(solution)/shard_map/all_to_all | solution.py:215
  140.1 0.9 shard_map.73
  (13 shorter events, 0.1 us)
Async XLA Ops:
  1.7 11.4 %collective-permute-start.1 = (f32[4,2,48,128]{3,2,1,0:T(8,128)S(1)}, f32[4,2,48,128]{3,2,1,0:T(8,128)S(1)}, u32[]{:S(2)}, u32[]{:S(2)}) collective-permute-start(f32[4,2,48,128]{3,2,1,0:T(8,128)S(1)} %get-tuple-element.35), channel_id=1, source_target_pairs={{1,0},{2,1},{3,2},{4,3},{5,4},{6,5},{7,6},{0,7},{9,8},{10,9},{11,1... | collective-permute-start | bytes 589832 | tf_op jit(solution)/shard_map/ppermute | solution.py:227
  6.7 8.8 %collective-permute-start = (f32[4,2,48,128]{3,2,1,0:T(8,128)S(1)}, f32[4,2,48,128]{3,2,1,0:T(8,128)S(1)}, u32[]{:S(2)}, u32[]{:S(2)}) collective-permute-start(f32[4,2,48,128]{3,2,1,0:T(8,128)S(1)} %get-tuple-element.36), channel_id=1, source_target_pairs={{0,1},{1,2},{2,3},{3,4},{4,5},{5,6},{6,7},{7,0},{8,9},{9,10},{10,1... | collective-permute-start | bytes 589832 | tf_op jit(solution)/shard_map/ppermute | solution.py:227
  6.7 1.3 copy-start
  8.0 1.0 copy-start.2
  9.0 0.9 copy-start.3
  9.8 0.7 copy-start.5
  17.2 52.9 %all-to-all-start = ((f32[32,96,128]{2,1,0:T(8,128)}), f32[32,96,128]{2,1,0:T(8,128)S(1)}, u32[]{:S(2)}, u32[]{:S(2)}) async-start(f32[32,96,128]{2,1,0:T(8,128)} %get-tuple-element.23), calls=%async_computation | async-start | bytes 3145728 | tf_op jit(solution)/shard_map/all_to_all | solution.py:215
  29.3 51.9 %collective-permute-start.2 = (f32[12,2,48,128]{3,2,1,0:T(8,128)S(1)}, f32[12,2,48,128]{3,2,1,0:T(8,128)S(1)}, u32[]{:S(2)}, u32[]{:S(2)}) collective-permute-start(f32[12,2,48,128]{3,2,1,0:T(8,128)S(1)} %get-tuple-element.27), channel_id=1, source_target_pairs={{0,1},{1,0},{2,3},{3,2},{4,5},{5,4},{6,7},{7,6},{8,9},{9,8},{10,11... | collective-permute-start | bytes 1769480 | tf_op jit(solution)/shard_map/ppermute | solution.py:298
  81.9 14.1 %all-to-all-start.2 = ((f32[16,24,128]{2,1,0:T(8,128)}), f32[16,24,128]{2,1,0:T(8,128)S(1)}, u32[]{:S(2)}, u32[]{:S(2)}) async-start(f32[16,24,128]{2,1,0:T(8,128)} %broadcast_in_dim.4), calls=%async_computation.2 | async-start | bytes 393216 | tf_op jit(solution)/shard_map/all_to_all | solution.py:215
  87.0 20.9 %collective-permute-start.3 = (f32[12,2,48,128]{3,2,1,0:T(8,128)}, f32[12,2,48,128]{3,2,1,0:T(8,128)}, u32[]{:S(2)}, u32[]{:S(2)}) collective-permute-start(f32[12,2,48,128]{3,2,1,0:T(8,128)} %get-tuple-element.31), channel_id=1, source_target_pairs={{0,1},{1,0},{2,3},{3,2},{4,5},{5,4},{6,7},{7,6},{8,9},{9,8},{10,11... | collective-permute-start | bytes 1769480 | tf_op jit(solution)/shard_map/ppermute | solution.py:301
  106.2 28.7 %copy-start.1 = (f32[12,4,48,128]{3,2,1,0:T(8,128)S(1)}, f32[12,4,48,128]{3,2,1,0:T(8,128)}, u32[]{:S(2)}) copy-start(f32[12,4,48,128]{3,2,1,0:T(8,128)} %field_ref.3) | copy-start | bytes 3538948
  106.2 28.8 %copy-start.4 = (f32[4,48,128]{2,1,0:T(8,128)S(1)}, f32[4,48,128]{2,1,0:T(8,128)}, u32[]{:S(2)}) copy-start(f32[4,48,128]{2,1,0:T(8,128)} %pot_ref.3) | copy-start | bytes 294916
  107.9 22.1 %all-to-all-start.4 = ((f32[32,24,128]{2,1,0:T(8,128)}), f32[32,24,128]{2,1,0:T(8,128)S(1)}, u32[]{:S(2)}, u32[]{:S(2)}) async-start(f32[32,24,128]{2,1,0:T(8,128)} %bitcast.2), calls=%async_computation.4 | async-start | bytes 786432 | tf_op jit(solution)/shard_map/all_to_all | solution.py:215
  114.7 20.2 %collective-permute-start.4 = (f32[12,2,48,128]{3,2,1,0:T(8,128)}, f32[12,2,48,128]{3,2,1,0:T(8,128)S(1)}, u32[]{:S(2)}, u32[]{:S(2)}) collective-permute-start(f32[12,2,48,128]{3,2,1,0:T(8,128)} %collective-permute-done.3), channel_id=1, source_target_pairs={{0,2},{1,7},{2,4},{3,1},{4,6},{5,3},{6,0},{7,5},{8,10},{9,15},{10,... | collective-permute-start | bytes 1769480 | tf_op jit(solution)/shard_map/ppermute | solution.py:314
  130.6 9.4 %all-to-all-start.5 = ((f32[8,8,128]{2,1,0:T(8,128)}), f32[8,8,128]{2,1,0:T(8,128)S(1)}, u32[]{:S(2)}, u32[]{:S(2)}) async-start(f32[8,8,128]{2,1,0:T(8,128)} %shard_map.72), calls=%async_computation.5 | async-start | bytes 65536 | tf_op jit(solution)/shard_map/all_to_all | solution.py:215
